TPU v7x, 512 devices: a whole 4x8x8 slice. The times are simulated.
512 devices in a mesh: sample: 16 (over y, core), atom: 32 (over x, z).
Axes of the slice: x: 4, y: 8, z: 8, core: 2. Of those that a mesh axis runs over, the one named last changes fastest.
Arguments:
- positions: float32 [3, 131072], P(None, ('sample', 'atom')), parts along dimension 1, may hold values from -6 to 6
- fresh_noise: float32 [3, 131072], P(None, ('sample', 'atom')), parts along dimension 1, may hold values from -6 to 6
- timestep: int32 [1], replicated, may hold values from 0 to 199
- atom_single: bfloat16 [8192, 128], P('atom'), may hold values from -6 to 6
- pos_weight: float32 [3, 128], replicated, may hold values from -3.5 to 3.5
- ln_gain: float32 [2, 2, 128], replicated, may hold values from 0.1 to 1.9
- w_query: bfloat16 [2, 128, 128], replicated
- w_key: bfloat16 [2, 128, 128], replicated
- w_value: bfloat16 [2, 128, 128], replicated, may hold values from -0.5 to 0.5
- w_out: bfloat16 [2, 128, 128], replicated, may hold values from -0.5 to 0.5
- w_gate_up: bfloat16 [2, 128, 512], replicated, may hold values from -0.5 to 0.5
- w_down: bfloat16 [2, 256, 128], replicated, may hold values from -0.375 to 0.375
- w_head: float32 [3, 128], replicated, may hold values from -0.5 to 0.5
- key_window: int32 [64, 8], P('atom'), may hold values from 0 to 63, as said below
- block_pairs: int32 [2, 2048], P(None, 'atom'), may hold values from 0 to 63, as said below
- pair_count: int32 [32], P('atom'), may hold values from 0 to 64, as said below
- bond_atoms: int32 [2, 64, 128], P(None, 'atom'), may hold values from 0 to 127
Outputs:
- next_positions: float32 [3, 131072], P(None, ('sample', 'atom')), parts along dimension 1
There are 16 independent parts, one for each index of `sample`. A program takes and returns all parts, laid end to end along the dimension named above; an argument that names none is the same for every part. Nothing has to cross between parts.
Inputs may be any that keep to these rules, and one draw needn't show every extreme that they name: `key_window`: every entry lies within 2 blocks of its row's block; in every row both distances 2 below and above are used where the grid has them, and the row's own block is in it. `block_pairs`: the two blocks of a column differ. Among the live columns of one owner, at most 6 of the entries of both rows together name blocks of one device (blocks d * 2 to (d + 1) * 2 - 1), and the owner with 64 live columns has exactly 6 on some device. `pair_count`: the entries sum to exactly 512.
All inputs are finite; a program needn't handle non-finite values.
Results may differ from a plain program's by a relative error of at most 0.0015.
Values may be sent and summed in bfloat16 or wider, within the bound.
No kernel may reach another device: no remote copies, remote signals or barrier semaphores. Data moves between devices by JAX's collectives and lax.ppermute only.
A program may use at most 64 MiB of HBM per device.

v0:
```python
import functools
import math

import jax
import jax.numpy as jnp
from jax import lax
from jax.experimental import pallas as pl
from jax.experimental.pallas import tpu as pltpu
from jax.sharding import PartitionSpec as P

HEADS = 4
LANES = 128
ROWS = 256
VMEM_GRANT = 60 * 1024 * 1024
VMEM_SMALL = 16 * 1024 * 1024
NORM_EPS = 1e-05
STEER = 0.3
ABSENT = -(2.0**120)
LOG2E = 1.4426950408889634
KAPPA = 2.0 * math.sqrt(LOG2E)

f32 = jnp.float32
bf16 = jnp.bfloat16


def pack_kernel(count_ref, tile_ref, out_ref):
    shape = tile_ref.shape
    row = lax.broadcasted_iota(jnp.int32, shape, 0)
    lane = lax.broadcasted_iota(jnp.int32, shape, 1)
    dead = (row == 6) & (lane % 64 >= count_ref[0])
    out_ref[...] = jnp.broadcast_to(jnp.where(dead, -1.0, tile_ref[...])[None], out_ref.shape)


def split3(values):
    high = values.astype(bf16)
    rest = values - high.astype(f32)
    mid = rest.astype(bf16)
    low = (rest - mid.astype(f32)).astype(bf16)
    return jnp.concatenate([high, mid, low], axis=0)


def join3(values):
    rows = values.shape[0] // 3
    return values[:rows] + values[rows : 2 * rows] + values[2 * rows :]


def norm_columns(values):
    center = values - jnp.mean(values, axis=0, keepdims=True)
    spread = jnp.mean(center * center, axis=0, keepdims=True)
    return center * lax.rsqrt(spread + NORM_EPS)


def dot_t(left, right):
    return lax.dot_general(left, right, (((0,), (0,)), ((), ())), preferred_element_type=f32)


def dot_nt(left, right):
    return lax.dot_general(left, right, (((1,), (1,)), ((), ())), preferred_element_type=f32)


def dot(left, right):
    return jnp.dot(left, right, preferred_element_type=f32)


def bond_kernel(positions_ref, bonds_ref, out_ref):
    positions = jnp.concatenate([positions_ref[...], jnp.zeros((5, 2 * LANES), f32)], axis=0)

    forces = []
    atom_id = lax.broadcasted_iota(jnp.int32, (LANES, LANES), 0)
    for block in range(2):
        incidence = (
            (atom_id == bonds_ref[0, block : block + 1, :]).astype(f32)
            - (atom_id == bonds_ref[1, block : block + 1, :]).astype(f32)
        ).astype(bf16)
        offset = join3(dot(split3(positions[:, block * LANES : (block + 1) * LANES]), incidence))
        stretch = jnp.sum(offset * offset, axis=0, keepdims=True) - 1.0
        pull = (-0.2 * stretch) * offset
        forces.append(join3(dot_nt(split3(pull), incidence)))
    out_ref[...] = jnp.concatenate(forces, axis=1)


def force_kernel(first_ref, tiles_ref, positions_ref, bond_ref, out_ref, spread_own, push, list_v, bias_v, list_s, bias_s, sems):
    me = first_ref[0]

    codes = tiles_ref[:, 6, :].astype(jnp.int32)
    half = lax.broadcasted_iota(jnp.int32, codes.shape, 1) // 64
    mine = me * 2 + half
    first = jnp.where(codes < 0, -1, codes // 64)
    second = jnp.where(codes < 0, -1, codes % 64)
    partner = jnp.where(first == mine, second, jnp.where(second == mine, first, -1)).astype(f32)
    block_id = lax.broadcasted_iota(jnp.int32, (64, LANES), 0).astype(f32)
    hits = jnp.zeros((64, LANES), f32)
    for row in range(codes.shape[0]):
        hits = hits + jnp.where(partner[row : row + 1] == block_id, 1.0, 0.0)
    row_half = lax.broadcasted_iota(jnp.int32, (LANES, LANES), 0) // 64
    col_half = lax.broadcasted_iota(jnp.int32, (LANES, LANES), 1) // 64
    count = dot(hits.astype(bf16), (row_half == col_half).astype(bf16))
    present = count > 0.5
    lower = lax.broadcasted_iota(jnp.int32, (64, 64), 1) < lax.broadcasted_iota(jnp.int32, (64, 64), 0)
    rank = dot(lower.astype(bf16), present.astype(bf16))
    slot = (lax.broadcasted_iota(jnp.int32, (64, LANES), 1) % 64).astype(f32)
    chosen = present & (rank == slot)
    listed = jnp.sum(jnp.where(chosen, block_id, 0.0), axis=0, keepdims=True)
    times = jnp.sum(jnp.where(chosen, count, 0.0), axis=0, keepdims=True)
    total = jnp.sum(present.astype(f32), axis=0, keepdims=True)
    list_v[0:1, :] = listed.astype(jnp.int32)
    list_v[1:2, :] = total.astype(jnp.int32)
    bias_v[0:1, :] = jnp.where(times > 0.5, jnp.log2(jnp.maximum(times, 1.0)), ABSENT)
    list_copy = pltpu.make_async_copy(list_v, list_s, sems.at[0])
    bias_copy = pltpu.make_async_copy(bias_v, bias_s, sems.at[1])
    list_copy.start()
    bias_copy.start()

    for block in range(2):
        for comp in range(3):
            row = positions_ref[comp : comp + 1, block * LANES : (block + 1) * LANES] * KAPPA
            spread_own[3 * block + comp] = jnp.broadcast_to(row, (LANES, LANES)).T
            push[3 * block + comp] = jnp.zeros((LANES, LANES), f32)

    forces = []
    list_copy.wait()
    bias_copy.wait()
    for block in range(2):

        def one_pair(index, carry, block=block):
            partners = []
            for sub in range(2):
                entry = block * 64 + 2 * index + sub
                partner = list_s[0, entry]
                device = partner // 2
                within = partner % 2
                rows = [
                    tiles_ref[device, pl.ds(2 * comp + within, 1), :] * KAPPA for comp in range(3)
                ]
                partners.append((rows, bias_s[0, entry]))
            for group in range(0, LANES, 8):
                own = [spread_own[3 * block + comp, group : group + 8, :] for comp in range(3)]
                sums = [push[3 * block + comp, group : group + 8, :] for comp in range(3)]
                for rows, bias in partners:
                    offset = [own[comp] - rows[comp] for comp in range(3)]
                    power = bias - offset[0] * offset[0]
                    power = power - offset[1] * offset[1]
                    power = power - offset[2] * offset[2]
                    weight = jnp.exp2(power)
                    sums = [sums[comp] + weight * offset[comp] for comp in range(3)]
                for comp in range(3):
                    push[3 * block + comp, group : group + 8, :] = sums[comp]
            return carry

        lax.fori_loop(0, (list_s[1, block * 64] + 1) // 2, one_pair, 0)
        rows = [jnp.sum(push[3 * block + comp].T, axis=0, keepdims=True) for comp in range(3)]
        clash = jnp.concatenate(rows + [jnp.zeros((5, LANES), f32)], axis=0)
        forces.append(clash * (8.0 / KAPPA))
    out_ref[...] = bond_ref[...] + jnp.concatenate(forces, axis=1)


def start_copies(sources, targets, sems):
    copies = [
        pltpu.make_async_copy(source, target, sems.at[index])
        for index, (source, target) in enumerate(zip(sources, targets))
    ]
    for copy in copies:
        copy.start()
    return copies


def prepare_kernel(*refs):
    first_ref, sources, (stream_ref, normed_ref, rows_ref, tile_ref) = refs[0], refs[1:8], refs[8:12]
    targets, sems = refs[12:19], refs[19]
    time_ref, positions_ref, single_ref, pos_weight_ref, gain_ref, pairs_ref, window_ref = targets
    for copy in start_copies(sources, targets, sems):
        copy.wait()
    level = 0.2 + 0.02 * jnp.full((1, ROWS), time_ref[0], jnp.int32).astype(f32)
    spread_sq = level * level + 1.0
    c_input = 1.0 / jnp.sqrt(spread_sq)
    window = window_ref[...]
    own = first_ref[0] * 2 + lax.broadcasted_iota(jnp.int32, window.shape, 0)
    lane = lax.broadcasted_iota(jnp.int32, (1, ROWS), 1)
    counts = jnp.zeros((1, ROWS), f32)
    for offset in range(5):
        hit = jnp.sum((window == own + (offset - 2)).astype(f32), axis=1, keepdims=True)
        counts = jnp.where(lane == offset, hit[0:1], counts)
        counts = jnp.where(lane == 8 + offset, hit[1:2], counts)
    counts = jnp.where(counts > 0.0, jnp.log2(jnp.maximum(counts, 1.0)), ABSENT)
    gain_rows = [
        jnp.concatenate([gain_ref[layer, 0:1], gain_ref[layer, 1:2]], axis=1) for layer in range(2)
    ]
    rows_ref[...] = jnp.concatenate(
        [level, spread_sq, c_input] + gain_rows + [counts, jnp.zeros((2, ROWS), f32)], axis=0
    )
    for row in range(6):
        part = slice((row % 2) * LANES, (row % 2 + 1) * LANES)
        tile_ref[row : row + 1, :] = positions_ref[row // 2 : row // 2 + 1, part]
    pairs = pairs_ref[...]
    codes = (pairs[0:1] * 64 + pairs[1:2]).astype(f32)
    tile_ref[6:7, :] = jnp.concatenate([codes, codes], axis=1)
    tile_ref[7:8, :] = jnp.zeros((1, LANES), f32)
    columns = jnp.concatenate(
        [pos_weight_ref[...], gain_ref[0, 0:1], jnp.zeros((4, LANES), f32)], axis=0
    ).T
    identity = (
        lax.broadcasted_iota(jnp.int32, (LANES, LANES), 0)
        == lax.broadcasted_iota(jnp.int32, (LANES, LANES), 1)
    ).astype(f32).astype(bf16)
    stream = dot_nt(identity, single_ref[...])
    for comp in range(3):
        stream = stream + columns[:, comp : comp + 1] * (positions_ref[comp : comp + 1, :] * c_input)
    stream_ref[...] = stream
    normed_ref[...] = (norm_columns(stream) * columns[:, 3:4]).astype(bf16).T


def layer_values(layer, first_ref, halo, stream_ref, rows_ref, weights, scratch):
    even_ref, own_ref, odd_ref = halo
    w_query_ref, w_key_ref, w_value_ref, w_out_ref, w_gate_up_ref, w_down_ref = weights
    near, keys, values, attended = scratch
    head_size = LANES // HEADS
    query_scale = LOG2E * head_size ** -0.5
    near[ROWS : 2 * ROWS, :] = own_ref[...]

    @pl.when(first_ref[0] % 2 == 0)
    def _():
        near[:ROWS, :] = odd_ref[...]
        near[2 * ROWS :, :] = even_ref[...]

    @pl.when(first_ref[0] % 2 == 1)
    def _():
        near[:ROWS, :] = even_ref[...]
        near[2 * ROWS :, :] = odd_ref[...]

    row_block = lax.broadcasted_iota(jnp.int32, (3 * ROWS, LANES), 0) // LANES
    lane = lax.broadcasted_iota(jnp.int32, (3 * ROWS, LANES), 1)
    keys[:, LANES:] = jnp.where((lane % 16 == row_block) & (lane < 32), 1.0, 0.0).astype(bf16)
    window = rows_ref[5:6, :LANES]
    rows = []
    for chunk in range(6):
        sides = []
        for block in range(2):
            offset = chunk - block
            if 0 <= offset < 5:
                lane_id = block * 8 + offset
                sides.append(jnp.broadcast_to(window[:, lane_id : lane_id + 1], (1, LANES)))
            else:
                sides.append(jnp.full((1, LANES), ABSENT, f32))
        rows.append(jnp.concatenate(sides, axis=1))
    rows = jnp.concatenate(rows + [jnp.zeros((10, ROWS), f32)], axis=0)
    high = rows.astype(bf16)
    low = (rows - high.astype(f32)).astype(bf16)
    bias = jnp.concatenate([high, low, jnp.zeros((LANES - 32, ROWS), bf16)], axis=0)

    keys[:, :LANES] = dot(near[...], w_key_ref[layer]).astype(bf16)
    query_t = (dot_nt(w_query_ref[layer].T, own_ref[...]) * query_scale).astype(bf16)
    value_t = dot_nt(w_value_ref[layer].T, near[...]).astype(bf16)
    for head in range(HEADS):
        values[head * 48 : head * 48 + 32, :] = value_t[head * 32 : head * 32 + 32]
        values[head * 48 + 32 : head * 48 + 48, :] = jnp.ones((16, 3 * ROWS), bf16)

    def attend(exact):
        pieces = []
        sums = []

        def scores_of(head):
            parts = []
            if head:
                parts.append(jnp.zeros((head * head_size, ROWS), bf16))
            parts.append(query_t[head * head_size : (head + 1) * head_size])
            if head < HEADS - 1:
                parts.append(jnp.zeros(((HEADS - 1 - head) * head_size, ROWS), bf16))
            return dot(keys[...], jnp.concatenate(parts + [bias], axis=0))

        following = scores_of(0)
        for head in range(HEADS):
            scores = following
            if head < HEADS - 1:
                following = scores_of(head + 1)
            if exact:
                scores = scores - jnp.max(scores, axis=0, keepdims=True)
            blank = jnp.zeros((LANES, LANES), bf16)
            weights_t = jnp.concatenate(
                [
                    jnp.concatenate([jnp.exp2(scores[: 5 * LANES, :LANES]).astype(bf16), blank], axis=0),
                    jnp.concatenate([blank, jnp.exp2(scores[LANES:, LANES:]).astype(bf16)], axis=0),
                ],
                axis=1,
            )
            mixed = dot(values[head * 48 : (head + 1) * 48, :], weights_t)
            total = mixed[head_size : head_size + 1]
            sums.append(total)
            pieces.append(mixed[:head_size] * (1.0 / total))
        attended[...] = jnp.concatenate(pieces, axis=0).astype(bf16)
        return jnp.concatenate(sums, axis=0)

    sums = attend(False)
    safe = (jnp.min(sums) > 2.0**-80) & (jnp.max(sums) < 2.0**100)

    @pl.when(jnp.logical_not(safe))
    def _():
        attend(True)

    gains = jnp.concatenate(
        [rows_ref[3 + index // 2 : 4 + index // 2, (index % 2) * LANES : (index % 2 + 1) * LANES] for index in range(4)]
        + [jnp.zeros((4, LANES), f32)],
        axis=0,
    ).T
    now = stream_ref[...] + dot(w_out_ref[layer].T, attended[...])
    normed = (norm_columns(now) * gains[:, 2 * layer + 1 : 2 * layer + 2]).astype(bf16)
    gate_up = dot(w_gate_up_ref[layer].T, normed)
    width = gate_up.shape[0] // 2
    half, up = 0.5 * gate_up[:width], gate_up[width:]
    hidden = ((half + half * jnp.tanh(half)) * up).astype(bf16)
    return now + dot(w_down_ref[layer].T, hidden), gains


def first_layer_kernel(first_ref, even_ref, own_ref, odd_ref, stream_ref, rows_ref, *refs):
    weights, (out_ref, normed_ref), scratch = refs[:6], refs[6:8], refs[8:]
    stream, gains = layer_values(
        0, first_ref, (even_ref, own_ref, odd_ref), stream_ref, rows_ref, weights, scratch
    )
    out_ref[...] = stream
    normed_ref[...] = (norm_columns(stream) * gains[:, 2:3]).astype(bf16).T


def last_layer_kernel(first_ref, even_ref, own_ref, odd_ref, stream_ref, rows_ref, *refs):
    weights, (positions_ref, noise_ref, force_ref, w_head_ref) = refs[:6], refs[6:10]
    out_ref, scratch = refs[10], refs[11:]
    stream, _ = layer_values(
        1, first_ref, (even_ref, own_ref, odd_ref), stream_ref, rows_ref, weights, scratch
    )
    final = norm_columns(stream)
    head_rows = jnp.concatenate([w_head_ref[...], jnp.zeros((5, LANES), f32)], axis=0)
    update = jnp.dot(head_rows, final, precision=lax.Precision.HIGHEST, preferred_element_type=f32)
    level, spread_sq, c_input = rows_ref[0:1], rows_ref[1:2], rows_ref[2:3]
    positions = jnp.concatenate([positions_ref[...], jnp.zeros((5, ROWS), f32)], axis=0)
    fresh = jnp.concatenate([noise_ref[...], jnp.zeros((5, ROWS), f32)], axis=0)
    denoised = positions * (1.0 / spread_sq) + (level * c_input) * update
    following = 0.85 * level
    result = denoised + STEER * force_ref[...] + following * (0.8 * (positions - denoised) / level + 0.6 * fresh)
    out_ref[...] = result[:3]


def body(
    positions,
    fresh_noise,
    timestep,
    atom_single,
    pos_weight,
    ln_gain,
    w_query,
    w_key,
    w_value,
    w_out,
    w_gate_up,
    w_down,
    w_head,
    key_window,
    block_pairs,
    pair_count,
    bond_atoms,
):
    devices = lax.axis_size("atom")
    first = lax.axis_index("atom").astype(jnp.int32).reshape(1)
    smem = pl.BlockSpec(memory_space=pltpu.SMEM)
    vmem = pl.BlockSpec(memory_space=pltpu.VMEM)
    hbm = pl.BlockSpec(memory_space=pltpu.HBM)
    rows = atom_single.shape[0]

    def from_neighbours(array):
        even = [(i, i ^ 1) for i in range(devices)]
        odd = [(i, ((i + 1) ^ 1) - 1) for i in range(1, devices - 1)]
        return lax.ppermute(array, "atom", even), lax.ppermute(array, "atom", odd)

    stream, normed, schedule, tile = pl.pallas_call(
        prepare_kernel,
        out_shape=(
            jax.ShapeDtypeStruct((LANES, rows), f32),
            jax.ShapeDtypeStruct((rows, LANES), bf16),
            jax.ShapeDtypeStruct((8, rows), f32),
            jax.ShapeDtypeStruct((8, LANES), f32),
        ),
        in_specs=[smem] + [hbm] * 7,
        out_specs=(vmem,) * 4,
        scratch_shapes=[
            pltpu.SMEM(timestep.shape, jnp.int32),
            pltpu.VMEM(positions.shape, f32),
            pltpu.VMEM(atom_single.shape, bf16),
            pltpu.VMEM(pos_weight.shape, f32),
            pltpu.VMEM(ln_gain.shape, f32),
            pltpu.VMEM(block_pairs.shape, jnp.int32),
            pltpu.VMEM(key_window.shape, jnp.int32),
            pltpu.SemaphoreType.DMA((7,)),
        ],
        compiler_params=pltpu.CompilerParams(vmem_limit_bytes=VMEM_GRANT),
    )(first, timestep, positions, atom_single, pos_weight, ln_gain, block_pairs, key_window)
    even, odd = from_neighbours(normed)

    packed = pl.pallas_call(
        pack_kernel,
        out_shape=jax.ShapeDtypeStruct((devices, 8, LANES), f32),
        in_specs=[smem, vmem],
        out_specs=vmem,
        cost_estimate=pl.CostEstimate(flops=40_000_000, bytes_accessed=10_000_000, transcendentals=1_000_000),
        compiler_params=pltpu.CompilerParams(vmem_limit_bytes=VMEM_SMALL),
    )(pair_count, tile)
    tiles = lax.all_to_all(packed, "atom", 0, 0)

    weights = (w_query, w_key, w_value, w_out, w_gate_up, w_down)
    layer_scratch = [
        pltpu.VMEM((3 * rows, LANES), bf16),
        pltpu.VMEM((3 * rows, 2 * LANES), bf16),
        pltpu.VMEM((HEADS * 48, 3 * rows), bf16),
        pltpu.VMEM((LANES, rows), bf16),
    ]
    layer_cost = pl.CostEstimate(flops=2_000_000_000, bytes_accessed=20_000_000, transcendentals=2_000_000)
    stream, normed = pl.pallas_call(
        first_layer_kernel,
        out_shape=(
            jax.ShapeDtypeStruct((LANES, rows), f32),
            jax.ShapeDtypeStruct((rows, LANES), bf16),
        ),
        in_specs=[smem] + [vmem] * 11,
        out_specs=(vmem, vmem),
        scratch_shapes=layer_scratch,
        cost_estimate=layer_cost,
        compiler_params=pltpu.CompilerParams(vmem_limit_bytes=VMEM_SMALL),
    )(first, even, normed, odd, stream, schedule, *weights)
    even, odd = from_neighbours(normed)

    bond_force = pl.pallas_call(
        bond_kernel,
        out_shape=jax.ShapeDtypeStruct((8, 2 * LANES), f32),
        in_specs=[vmem, vmem],
        out_specs=vmem,
        cost_estimate=pl.CostEstimate(flops=80_000_000, bytes_accessed=8_000_000, transcendentals=0),
        compiler_params=pltpu.CompilerParams(vmem_limit_bytes=VMEM_SMALL),
    )(positions, bond_atoms)

    force = pl.pallas_call(
        force_kernel,
        out_shape=jax.ShapeDtypeStruct((8, 2 * LANES), f32),
        in_specs=[smem, vmem, vmem, vmem],
        out_specs=vmem,
        scratch_shapes=[
            pltpu.VMEM((6, LANES, LANES), f32),
            pltpu.VMEM((6, LANES, LANES), f32),
            pltpu.VMEM((8, LANES), jnp.int32),
            pltpu.VMEM((8, LANES), f32),
            pltpu.SMEM((8, LANES), jnp.int32),
            pltpu.SMEM((8, LANES), f32),
            pltpu.SemaphoreType.DMA((2,)),
        ],
        cost_estimate=pl.CostEstimate(flops=80_000_000, bytes_accessed=16_000_000, transcendentals=2_000_000),
        compiler_params=pltpu.CompilerParams(vmem_limit_bytes=VMEM_SMALL),
    )(first, tiles, positions, bond_force)

    return pl.pallas_call(
        last_layer_kernel,
        out_shape=jax.ShapeDtypeStruct(positions.shape, f32),
        in_specs=[smem] + [vmem] * 15,
        out_specs=vmem,
        scratch_shapes=layer_scratch,
        cost_estimate=layer_cost,
        compiler_params=pltpu.CompilerParams(vmem_limit_bytes=VMEM_SMALL),
    )(
        first,
        even,
        normed,
        odd,
        stream,
        schedule,
        *weights,
        positions,
        fresh_noise,
        force,
        w_head,
    )


def solution(mesh):
    in_specs = (
        P(None, ("sample", "atom")),
        P(None, ("sample", "atom")),
        P(),
        P("atom", None),
        P(),
        P(),
        P(),
        P(),
        P(),
        P(),
        P(),
        P(),
        P(),
        P("atom", None),
        P(None, "atom"),
        P("atom"),
        P(None, "atom", None),
    )
    out_specs = P(None, ("sample", "atom"))
    return jax.shard_map(body, mesh=mesh, in_specs=in_specs, out_specs=out_specs, check_vma=False)
```

profile of v0, /device:TPU:6, one launch (start us, length us, event | category | flops | bytes accessed | tf_op | source)
XLA Modules:
  0.0 43.6 jit_solution(6465585132047336463)
XLA Ops:
  0.7 1.9 %shard_map.163 = (f32[128,256]{1,0:T(8,128)}, bf16[256,128]{1,0:T(8,128)(2,1)}, f32[8,256]{1,0:T(8,128)}, f32[8,128]{1,0:T(8,128)}) custom-call(s32[1]{0:T(128)} %bitcast.refs_0_.first_ref, s32[1]{0:T(128)S(6)} %copy.18.refs_1_, f32[3,256]{1,0:T(4,128)} %refs_6_.3, bf16[256,128]{1,0:T(8,128)(2,1)} %refs_3_.3, f32[3,128]{1,0:T(4,128)} %refs_4_.3, ...), custom_call_target="tpu_custom_call" | custom-call | tf_op jit(solution)/shard_map/pallas_call | solution.py:371
  2.6 0.0 copy-start.11
  2.6 4.3 %collective-permute-start = (bf16[256,128]{1,0:T(8,128)(2,1)}, bf16[256,128]{1,0:T(8,128)(2,1)S(1)}, u32[]{:S(2)}, u32[]{:S(2)}) collective-permute-start(bf16[256,128]{1,0:T(8,128)(2,1)} %get-tuple-element.11.own_ref), channel_id=1, source_target_pairs={{0,1},{1,0},{2,3},{3,2},{4,5},{5,4},{6,7},{7,6},{8,9},{9,8},{10,11... | collective-permute-start | bytes 196616 | tf_op jit(solution)/shard_map/ppermute | solution.py:369
  6.9 9.4 %collective-permute-start.1 = (bf16[256,128]{1,0:T(8,128)(2,1)}, bf16[256,128]{1,0:T(8,128)(2,1)S(1)}, u32[]{:S(2)}, u32[]{:S(2)}) collective-permute-start(bf16[256,128]{1,0:T(8,128)(2,1)} %get-tuple-element.11.own_ref), channel_id=1, source_target_pairs={{1,2},{2,1},{3,4},{4,3},{5,6},{6,5},{7,8},{8,7},{9,10},{10,9},{11,... | collective-permute-start | bytes 196616 | tf_op jit(solution)/shard_map/ppermute | solution.py:369
  17.0 0.0 copy-done.11
  17.0 0.0 copy-start.2
  17.0 0.0 copy-start.3
  17.0 0.0 copy-start.4
  17.0 0.0 copy-start.5
  17.0 0.0 copy-start.6
  17.0 0.0 copy-start.7
  17.0 0.0 copy-start.8
  17.0 0.0 copy-start.9
  17.1 0.7 %shard_map.165 = f32[32,8,128]{2,1,0:T(8,128)} custom-call(s32[1]{0:T(128)S(6)} %copy.19.count_ref, f32[8,128]{1,0:T(8,128)S(1)} %copy-done.11), custom_call_target="tpu_custom_call" | custom-call | flops 40000000 | bytes 10000000 | tf_op jit(solution)/shard_map/pallas_call | solution.py:395
  17.7 0.0 copy-start.1
  17.7 6.7 %all-to-all-start = ((f32[32,8,128]{2,1,0:T(8,128)}), f32[32,8,128]{2,1,0:T(8,128)S(1)}, u32[]{:S(2)}, u32[]{:S(2)}) async-start(f32[32,8,128]{2,1,0:T(8,128)} %shard_map.165), calls=%async_computation | async-start | bytes 262144 | tf_op jit(solution)/shard_map/all_to_all | solution.py:403
  24.4 0.0 collective-permute-done.even_ref
  24.4 0.0 collective-permute-done.1.odd_ref
  24.4 0.0 copy-done.2
  24.4 0.0 copy-done.3
  24.4 0.0 copy-done.4
  24.4 0.0 copy-done.5
  24.4 0.0 copy-done.6
  24.4 0.0 copy-done.7
  24.5 0.0 copy-done.8
  24.5 0.0 copy-done.9
  24.5 0.0 copy-done.1
  24.5 0.0 copy-start
  24.5 0.0 copy-start.12
  24.5 3.3 %shard_map.164 = (f32[128,256]{1,0:T(8,128)S(1)}, bf16[256,128]{1,0:T(8,128)(2,1)S(1)}) custom-call(s32[1]{0:T(128)} %bitcast.refs_0_.first_ref, bf16[256,128]{1,0:T(8,128)(2,1)S(1)} %collective-permute-done.even_ref, bf16[256,128]{1,0:T(8,128)(2,1)S(1)} %copy-done.8, bf16[256,128]{1,0:T(8,128)(2,1)S(1)} %collective-permute-done.1.odd_ref, ...), custom_call_target="tpu_custom_call" | custom-call | flops 2000000000 | bytes 20000000 | tf_op jit(solution)/shard_map/pallas_call | solution.py:413
  27.9 3.4 %collective-permute-start.2 = (bf16[256,128]{1,0:T(8,128)(2,1)S(1)}, bf16[256,128]{1,0:T(8,128)(2,1)S(1)}, u32[]{:S(2)}, u32[]{:S(2)}) collective-permute-start(bf16[256,128]{1,0:T(8,128)(2,1)S(1)} %get-tuple-element.14.own_ref), channel_id=1, source_target_pairs={{0,1},{1,0},{2,3},{3,2},{4,5},{5,4},{6,7},{7,6},{8,9},{9,8},{10,11... | collective-permute-start | bytes 196616 | tf_op jit(solution)/shard_map/ppermute | solution.py:369
  31.2 4.9 %collective-permute-start.3 = (bf16[256,128]{1,0:T(8,128)(2,1)S(1)}, bf16[256,128]{1,0:T(8,128)(2,1)S(1)}, u32[]{:S(2)}, u32[]{:S(2)}) collective-permute-start(bf16[256,128]{1,0:T(8,128)(2,1)S(1)} %get-tuple-element.14.own_ref), channel_id=1, source_target_pairs={{1,2},{2,1},{3,4},{4,3},{5,6},{6,5},{7,8},{8,7},{9,10},{10,9},{11,... | collective-permute-start | bytes 196616 | tf_op jit(solution)/shard_map/ppermute | solution.py:369
  36.1 0.0 copy-done
  36.1 0.0 copy-done.12
  36.1 0.3 shard_map.166.bond_ref
  36.4 0.0 copy-start.10
  36.4 0.0 copy-start.13
  36.4 0.0 all-to-all-done.tiles_ref
  36.4 2.8 %shard_map.167.refs_8_ = f32[8,256]{1,0:T(8,128)S(1)} custom-call(s32[1]{0:T(128)} %bitcast.refs_0_.first_ref, f32[32,8,128]{2,1,0:T(8,128)S(1)} %all-to-all-done.tiles_ref, f32[3,256]{1,0:T(4,128)S(1)} %copy-done, f32[8,256]{1,0:T(8,128)S(1)} %shard_map.166.bond_ref), custom_call_target="tpu_custom_call" | custom-call | flops 80000000 | bytes 16000000 | tf_op jit(solution)/shard_map/pallas_call | solution.py:436
  39.2 0.0 collective-permute-done.2.even_ref
  39.2 0.3 collective-permute-done.3.odd_ref
  39.5 0.0 copy-done.10
  39.5 0.0 copy-done.13
  39.5 4.1 %shard_map.168 = f32[3,256]{1,0:T(4,128)} custom-call(s32[1]{0:T(128)} %bitcast.refs_0_.first_ref, bf16[256,128]{1,0:T(8,128)(2,1)S(1)} %collective-permute-done.2.even_ref, bf16[256,128]{1,0:T(8,128)(2,1)S(1)} %get-tuple-element.14.own_ref, bf16[256,128]{1,0:T(8,128)(2,1)S(1)} %collective-permute-done.3.odd_ref, ...), custom_call_target="tpu_custom_call" | custom-call | flops 2000000000 | bytes 20000000 | tf_op jit(solution)/shard_map/pallas_call | solution.py:454
Async XLA Ops:
  2.6 14.3 %copy-start.11 = (f32[8,128]{1,0:T(8,128)S(1)}, f32[8,128]{1,0:T(8,128)}, u32[]{:S(2)}) copy-start(f32[8,128]{1,0:T(8,128)} %get-tuple-element.16.tile_ref) | copy-start | bytes 12292
  2.6 21.8 %collective-permute-start = (bf16[256,128]{1,0:T(8,128)(2,1)}, bf16[256,128]{1,0:T(8,128)(2,1)S(1)}, u32[]{:S(2)}, u32[]{:S(2)}) collective-permute-start(bf16[256,128]{1,0:T(8,128)(2,1)} %get-tuple-element.11.own_ref), channel_id=1, source_target_pairs={{0,1},{1,0},{2,3},{3,2},{4,5},{5,4},{6,7},{7,6},{8,9},{9,8},{10,11... | collective-permute-start | bytes 196616 | tf_op jit(solution)/shard_map/ppermute | solution.py:369
  6.9 17.5 %collective-permute-start.1 = (bf16[256,128]{1,0:T(8,128)(2,1)}, bf16[256,128]{1,0:T(8,128)(2,1)S(1)}, u32[]{:S(2)}, u32[]{:S(2)}) collective-permute-start(bf16[256,128]{1,0:T(8,128)(2,1)} %get-tuple-element.11.own_ref), channel_id=1, source_target_pairs={{1,2},{2,1},{3,4},{4,3},{5,6},{6,5},{7,8},{8,7},{9,10},{10,9},{11,... | collective-permute-start | bytes 196616 | tf_op jit(solution)/shard_map/ppermute | solution.py:369
  17.0 7.4 %copy-start.2 = (bf16[2,256,128]{2,1,0:T(8,128)(2,1)S(1)}, bf16[2,256,128]{2,1,0:T(8,128)(2,1)}, u32[]{:S(2)}) copy-start(bf16[2,256,128]{2,1,0:T(8,128)(2,1)} %refs_5_.5) | copy-start | bytes 393220
  17.0 7.4 %copy-start.3 = (f32[128,256]{1,0:T(8,128)S(1)}, f32[128,256]{1,0:T(8,128)}, u32[]{:S(2)}) copy-start(f32[128,256]{1,0:T(8,128)} %get-tuple-element.12.stream_ref) | copy-start | bytes 393220
  17.0 7.4 %copy-start.4 = (bf16[2,128,128]{2,1,0:T(8,128)(2,1)S(1)}, bf16[2,128,128]{2,1,0:T(8,128)(2,1)}, u32[]{:S(2)}) copy-start(bf16[2,128,128]{2,1,0:T(8,128)(2,1)} %refs_0_.3) | copy-start | bytes 196612
  17.0 7.4 %copy-start.5 = (bf16[2,128,128]{2,1,0:T(8,128)(2,1)S(1)}, bf16[2,128,128]{2,1,0:T(8,128)(2,1)}, u32[]{:S(2)}) copy-start(bf16[2,128,128]{2,1,0:T(8,128)(2,1)} %refs_1_.4) | copy-start | bytes 196612
  17.0 7.4 %copy-start.6 = (bf16[2,128,128]{2,1,0:T(8,128)(2,1)S(1)}, bf16[2,128,128]{2,1,0:T(8,128)(2,1)}, u32[]{:S(2)}) copy-start(bf16[2,128,128]{2,1,0:T(8,128)(2,1)} %refs_2_.5) | copy-start | bytes 196612
  17.0 7.4 %copy-start.7 = (bf16[2,128,128]{2,1,0:T(8,128)(2,1)S(1)}, bf16[2,128,128]{2,1,0:T(8,128)(2,1)}, u32[]{:S(2)}) copy-start(bf16[2,128,128]{2,1,0:T(8,128)(2,1)} %refs_3_.5) | copy-start | bytes 196612
  17.0 7.4 %copy-start.8 = (bf16[256,128]{1,0:T(8,128)(2,1)S(1)}, bf16[256,128]{1,0:T(8,128)(2,1)}, u32[]{:S(2)}) copy-start(bf16[256,128]{1,0:T(8,128)(2,1)} %get-tuple-element.11.own_ref) | copy-start | bytes 196612
  17.0 7.4 %copy-start.9 = (f32[8,256]{1,0:T(8,128)S(1)}, f32[8,256]{1,0:T(8,128)}, u32[]{:S(2)}) copy-start(f32[8,256]{1,0:T(8,128)} %get-tuple-element.13.rows_ref) | copy-start | bytes 24580
  17.7 6.8 %copy-start.1 = (bf16[2,128,512]{2,1,0:T(8,128)(2,1)S(1)}, bf16[2,128,512]{2,1,0:T(8,128)(2,1)}, u32[]{:S(2)}) copy-start(bf16[2,128,512]{2,1,0:T(8,128)(2,1)} %refs_4_.5) | copy-start | bytes 786436
  17.7 18.7 %all-to-all-start = ((f32[32,8,128]{2,1,0:T(8,128)}), f32[32,8,128]{2,1,0:T(8,128)S(1)}, u32[]{:S(2)}, u32[]{:S(2)}) async-start(f32[32,8,128]{2,1,0:T(8,128)} %shard_map.165), calls=%async_computation | async-start | bytes 262144 | tf_op jit(solution)/shard_map/all_to_all | solution.py:403
  24.5 11.6 %copy-start = (f32[3,256]{1,0:T(4,128)S(1)}, f32[3,256]{1,0:T(4,128)}, u32[]{:S(2)}) copy-start(f32[3,256]{1,0:T(4,128)} %refs_6_.3) | copy-start | bytes 9220
  24.5 11.6 %copy-start.12 = (s32[2,2,128]{2,1,0:T(2,128)S(1)}, s32[2,2,128]{2,1,0:T(2,128)}, u32[]{:S(2)}) copy-start(s32[2,2,128]{2,1,0:T(2,128)} %bonds_ref.1) | copy-start | bytes 6148
  27.9 11.4 %collective-permute-start.2 = (bf16[256,128]{1,0:T(8,128)(2,1)S(1)}, bf16[256,128]{1,0:T(8,128)(2,1)S(1)}, u32[]{:S(2)}, u32[]{:S(2)}) collective-permute-start(bf16[256,128]{1,0:T(8,128)(2,1)S(1)} %get-tuple-element.14.own_ref), channel_id=1, source_target_pairs={{0,1},{1,0},{2,3},{3,2},{4,5},{5,4},{6,7},{7,6},{8,9},{9,8},{10,11... | collective-permute-start | bytes 196616 | tf_op jit(solution)/shard_map/ppermute | solution.py:369
  31.2 8.3 %collective-permute-start.3 = (bf16[256,128]{1,0:T(8,128)(2,1)S(1)}, bf16[256,128]{1,0:T(8,128)(2,1)S(1)}, u32[]{:S(2)}, u32[]{:S(2)}) collective-permute-start(bf16[256,128]{1,0:T(8,128)(2,1)S(1)} %get-tuple-element.14.own_ref), channel_id=1, source_target_pairs={{1,2},{2,1},{3,4},{4,3},{5,6},{6,5},{7,8},{8,7},{9,10},{10,9},{11,... | collective-permute-start | bytes 196616 | tf_op jit(solution)/shard_map/ppermute | solution.py:369
  36.4 3.1 %copy-start.10 = (f32[3,256]{1,0:T(4,128)S(1)}, f32[3,256]{1,0:T(4,128)}, u32[]{:S(2)}) copy-start(f32[3,256]{1,0:T(4,128)} %refs_7_.3) | copy-start | bytes 9220
  36.4 3.1 %copy-start.13 = (f32[3,128]{1,0:T(4,128)S(1)}, f32[3,128]{1,0:T(4,128)}, u32[]{:S(2)}) copy-start(f32[3,128]{1,0:T(4,128)} %refs_9_.1) | copy-start | bytes 4612
where the time goes:
time: 43.9 us; the launch traced here: 43.6 us
  starting transfers between devices  28.6 us (65%)
  Pallas kernels  13.1 us (30%)
  between operations  1.59 us (4%)
    ppermute x4, starting transfers between devices, from_neighbours(): return (lax.ppermute(array, 'atom', even), lax.ppermute(array, 'atom', odd))  21.9 us
    all_to_all x1, starting transfers between devices, body(): tiles = lax.all_to_all(packed, 'atom', 0, 0)  6.65 us
    pallas_call x1, Pallas kernels, body(): pl.pallas_call(last_layer_kernel, out_shape=jax.ShapeDtypeStruct(position...  4.09 us
    pallas_call x1, Pallas kernels, body(): pl.pallas_call(first_layer_kernel, out_shape=(jax.ShapeDtypeStruct((LANES...  3.33 us
    pallas_call x1, Pallas kernels, body(): pl.pallas_call(force_kernel, out_shape=jax.ShapeDtypeStruct((8, 2 * LANES...  2.77 us
    pallas_call x1, Pallas kernels, body(): pl.pallas_call(prepare_kernel, out_shape=(jax.ShapeDtypeStruct((LANES, ro...  1.94 us
  transfers between devices with their start and end apart: 5, of which 1 were waited for; matrix products, arithmetic and copies ran while one was open for 0% of the time, Pallas kernels for 16%

commit v1 on v0

--- a/solution.py
+++ b/solution.py
@@ -62,24 +62,7 @@
     return jnp.dot(left, right, preferred_element_type=f32)
 
 
-def bond_kernel(positions_ref, bonds_ref, out_ref):
-    positions = jnp.concatenate([positions_ref[...], jnp.zeros((5, 2 * LANES), f32)], axis=0)
-
-    forces = []
-    atom_id = lax.broadcasted_iota(jnp.int32, (LANES, LANES), 0)
-    for block in range(2):
-        incidence = (
-            (atom_id == bonds_ref[0, block : block + 1, :]).astype(f32)
-            - (atom_id == bonds_ref[1, block : block + 1, :]).astype(f32)
-        ).astype(bf16)
-        offset = join3(dot(split3(positions[:, block * LANES : (block + 1) * LANES]), incidence))
-        stretch = jnp.sum(offset * offset, axis=0, keepdims=True) - 1.0
-        pull = (-0.2 * stretch) * offset
-        forces.append(join3(dot_nt(split3(pull), incidence)))
-    out_ref[...] = jnp.concatenate(forces, axis=1)
-
-
-def force_kernel(first_ref, tiles_ref, positions_ref, bond_ref, out_ref, spread_own, push, list_v, bias_v, list_s, bias_s, sems):
+def force_kernel(first_ref, tiles_ref, positions_ref, bonds_ref, out_ref, spread_own, push, list_v, bias_v, list_s, bias_s, sems):
     me = first_ref[0]
 
     codes = tiles_ref[:, 6, :].astype(jnp.int32)
@@ -117,7 +100,20 @@
             spread_own[3 * block + comp] = jnp.broadcast_to(row, (LANES, LANES)).T
             push[3 * block + comp] = jnp.zeros((LANES, LANES), f32)
 
+    positions = jnp.concatenate([positions_ref[...], jnp.zeros((5, 2 * LANES), f32)], axis=0)
+
     forces = []
+    atom_id = lax.broadcasted_iota(jnp.int32, (LANES, LANES), 0)
+    for block in range(2):
+        incidence = (
+            (atom_id == bonds_ref[0, block : block + 1, :]).astype(f32)
+            - (atom_id == bonds_ref[1, block : block + 1, :]).astype(f32)
+        ).astype(bf16)
+        offset = join3(dot(split3(positions[:, block * LANES : (block + 1) * LANES]), incidence))
+        stretch = jnp.sum(offset * offset, axis=0, keepdims=True) - 1.0
+        pull = (-0.2 * stretch) * offset
+        forces.append(join3(dot_nt(split3(pull), incidence)))
+
     list_copy.wait()
     bias_copy.wait()
     for block in range(2):
@@ -150,8 +146,8 @@
         lax.fori_loop(0, (list_s[1, block * 64] + 1) // 2, one_pair, 0)
         rows = [jnp.sum(push[3 * block + comp].T, axis=0, keepdims=True) for comp in range(3)]
         clash = jnp.concatenate(rows + [jnp.zeros((5, LANES), f32)], axis=0)
-        forces.append(clash * (8.0 / KAPPA))
-    out_ref[...] = bond_ref[...] + jnp.concatenate(forces, axis=1)
+        forces[block] = forces[block] + clash * (8.0 / KAPPA)
+    out_ref[...] = jnp.concatenate(forces, axis=1)
 
 
 def start_copies(sources, targets, sems):
@@ -209,7 +205,7 @@
     normed_ref[...] = (norm_columns(stream) * columns[:, 3:4]).astype(bf16).T
 
 
-def layer_values(layer, first_ref, halo, stream_ref, rows_ref, weights, scratch):
+def layer_values(layer, first_ref, halo, stream_ref, rows_ref, head_rows, weights, scratch):
     even_ref, own_ref, odd_ref = halo
     w_query_ref, w_key_ref, w_value_ref, w_out_ref, w_gate_up_ref, w_down_ref = weights
     near, keys, values, attended = scratch
@@ -298,7 +294,7 @@
 
     gains = jnp.concatenate(
         [rows_ref[3 + index // 2 : 4 + index // 2, (index % 2) * LANES : (index % 2 + 1) * LANES] for index in range(4)]
-        + [jnp.zeros((4, LANES), f32)],
+        + [head_rows],
         axis=0,
     ).T
     now = stream_ref[...] + dot(w_out_ref[layer].T, attended[...])
@@ -313,7 +309,7 @@
 def first_layer_kernel(first_ref, even_ref, own_ref, odd_ref, stream_ref, rows_ref, *refs):
     weights, (out_ref, normed_ref), scratch = refs[:6], refs[6:8], refs[8:]
     stream, gains = layer_values(
-        0, first_ref, (even_ref, own_ref, odd_ref), stream_ref, rows_ref, weights, scratch
+        0, first_ref, (even_ref, own_ref, odd_ref), stream_ref, rows_ref, jnp.zeros((4, LANES), f32), weights, scratch
     )
     out_ref[...] = stream
     normed_ref[...] = (norm_columns(stream) * gains[:, 2:3]).astype(bf16).T
@@ -322,12 +318,16 @@
 def last_layer_kernel(first_ref, even_ref, own_ref, odd_ref, stream_ref, rows_ref, *refs):
     weights, (positions_ref, noise_ref, force_ref, w_head_ref) = refs[:6], refs[6:10]
     out_ref, scratch = refs[10], refs[11:]
-    stream, _ = layer_values(
-        1, first_ref, (even_ref, own_ref, odd_ref), stream_ref, rows_ref, weights, scratch
+    head_rows = jnp.concatenate([w_head_ref[...], jnp.zeros((1, LANES), f32)], axis=0)
+    stream, columns = layer_values(
+        1, first_ref, (even_ref, own_ref, odd_ref), stream_ref, rows_ref, head_rows, weights, scratch
     )
     final = norm_columns(stream)
-    head_rows = jnp.concatenate([w_head_ref[...], jnp.zeros((5, LANES), f32)], axis=0)
-    update = jnp.dot(head_rows, final, precision=lax.Precision.HIGHEST, preferred_element_type=f32)
+    update = jnp.concatenate(
+        [jnp.sum(columns[:, 4 + comp : 5 + comp] * final, axis=0, keepdims=True) for comp in range(3)]
+        + [jnp.zeros((5, ROWS), f32)],
+        axis=0,
+    )
     level, spread_sq, c_input = rows_ref[0:1], rows_ref[1:2], rows_ref[2:3]
     positions = jnp.concatenate([positions_ref[...], jnp.zeros((5, ROWS), f32)], axis=0)
     fresh = jnp.concatenate([noise_ref[...], jnp.zeros((5, ROWS), f32)], axis=0)
@@ -424,15 +424,6 @@
     )(first, even, normed, odd, stream, schedule, *weights)
     even, odd = from_neighbours(normed)
 
-    bond_force = pl.pallas_call(
-        bond_kernel,
-        out_shape=jax.ShapeDtypeStruct((8, 2 * LANES), f32),
-        in_specs=[vmem, vmem],
-        out_specs=vmem,
-        cost_estimate=pl.CostEstimate(flops=80_000_000, bytes_accessed=8_000_000, transcendentals=0),
-        compiler_params=pltpu.CompilerParams(vmem_limit_bytes=VMEM_SMALL),
-    )(positions, bond_atoms)
-
     force = pl.pallas_call(
         force_kernel,
         out_shape=jax.ShapeDtypeStruct((8, 2 * LANES), f32),
@@ -449,7 +440,7 @@
         ],
         cost_estimate=pl.CostEstimate(flops=80_000_000, bytes_accessed=16_000_000, transcendentals=2_000_000),
         compiler_params=pltpu.CompilerParams(vmem_limit_bytes=VMEM_SMALL),
-    )(first, tiles, positions, bond_force)
+    )(first, tiles, positions, bond_atoms)
 
     return pl.pallas_call(
         last_layer_kernel,

time: 43.9 us -> 43.2 us (0.984)
  starting transfers between devices: 28.6 us -> 27.1 us
  waiting for transfers between devices: 0.3 us -> 1.3 us
    ppermute x4, starting transfers between devices: 21.9 us -> 19.9 us  [from_neighbours(): return (lax.ppermute(array, 'atom', even), lax.ppermute(array, 'atom', odd))]
    ppermute x4, waiting for transfers between devices: 0.3 us -> 1.29 us  [from_neighbours(): return (lax.ppermute(array, 'atom', even), lax.ppermute(array, 'atom', odd))]
    all_to_all x1, starting transfers between devices: 6.65 us -> 7.18 us  [body(): tiles = lax.all_to_all(packed, 'atom', 0, 0)]
where the time goes in v1:
time: 43.2 us; the launch traced here: 42.8 us
  starting transfers between devices  27.1 us (63%)
  Pallas kernels  12.7 us (29%)
  between operations  1.59 us (4%)
  waiting for transfers between devices  1.3 us (3%)
    ppermute x4, starting transfers between devices, from_neighbours(): return (lax.ppermute(array, 'atom', even), lax.ppermute(array, 'atom', odd))  19.9 us
    all_to_all x1, starting transfers between devices, body(): tiles = lax.all_to_all(packed, 'atom', 0, 0)  7.18 us
    pallas_call x1, Pallas kernels, body(): pl.pallas_call(last_layer_kernel, out_shape=jax.ShapeDtypeStruct(position...  3.91 us
    pallas_call x1, Pallas kernels, body(): pl.pallas_call(first_layer_kernel, out_shape=(jax.ShapeDtypeStruct((LANES...  3.34 us
    pallas_call x1, Pallas kernels, body(): pl.pallas_call(force_kernel, out_shape=jax.ShapeDtypeStruct((8, 2 * LANES...  2.9 us
    pallas_call x1, Pallas kernels, body(): pl.pallas_call(prepare_kernel, out_shape=(jax.ShapeDtypeStruct((LANES, ro...  1.94 us
    ppermute x4, waiting for transfers between devices, from_neighbours(): return (lax.ppermute(array, 'atom', even), lax.ppermute(array, 'atom', odd))  1.29 us
  transfers between devices with their start and end apart: 5, of which 1 were waited for; matrix products, arithmetic and copies ran while one was open for 0% of the time, Pallas kernels for 16%

profile of v1, /device:TPU:6, one launch (start us, length us, event | category | flops | bytes accessed | tf_op | source)
XLA Modules:
  0.0 42.8 jit_solution(17635525181065450184)
XLA Ops:
  0.7 1.9 %shard_map.163 = (f32[128,256]{1,0:T(8,128)}, bf16[256,128]{1,0:T(8,128)(2,1)}, f32[8,256]{1,0:T(8,128)}, f32[8,128]{1,0:T(8,128)}) custom-call(s32[1]{0:T(128)} %bitcast.refs_0_.first_ref, s32[1]{0:T(128)S(6)} %copy.18.refs_1_, f32[3,256]{1,0:T(4,128)} %refs_6_.3, bf16[256,128]{1,0:T(8,128)(2,1)} %refs_3_.3, f32[3,128]{1,0:T(4,128)} %refs_4_.3, ...), custom_call_target="tpu_custom_call" | custom-call | tf_op jit(solution)/shard_map/pallas_call | solution.py:371
  2.6 0.0 copy-start.11
  2.6 11.2 %collective-permute-start.1 = (bf16[256,128]{1,0:T(8,128)(2,1)}, bf16[256,128]{1,0:T(8,128)(2,1)S(1)}, u32[]{:S(2)}, u32[]{:S(2)}) collective-permute-start(bf16[256,128]{1,0:T(8,128)(2,1)} %get-tuple-element.11.own_ref), channel_id=1, source_target_pairs={{1,2},{2,1},{3,4},{4,3},{5,6},{6,5},{7,8},{8,7},{9,10},{10,9},{11,... | collective-permute-start | bytes 196616 | tf_op jit(solution)/shard_map/ppermute | solution.py:369
  13.8 1.9 %collective-permute-start = (bf16[256,128]{1,0:T(8,128)(2,1)}, bf16[256,128]{1,0:T(8,128)(2,1)S(1)}, u32[]{:S(2)}, u32[]{:S(2)}) collective-permute-start(bf16[256,128]{1,0:T(8,128)(2,1)} %get-tuple-element.11.own_ref), channel_id=1, source_target_pairs={{0,1},{1,0},{2,3},{3,2},{4,5},{5,4},{6,7},{7,6},{8,9},{9,8},{10,11... | collective-permute-start | bytes 196616 | tf_op jit(solution)/shard_map/ppermute | solution.py:369
  16.4 0.0 copy-done.11
  16.4 0.0 copy-start.2
  16.4 0.0 copy-start.3
  16.4 0.0 copy-start.4
  16.5 0.0 copy-start.5
  16.5 0.0 copy-start.6
  16.5 0.0 copy-start.7
  16.5 0.0 copy-start.8
  16.5 0.0 copy-start.9
  16.5 0.7 %shard_map.165 = f32[32,8,128]{2,1,0:T(8,128)} custom-call(s32[1]{0:T(128)S(6)} %copy.19.count_ref, f32[8,128]{1,0:T(8,128)S(1)} %copy-done.11), custom_call_target="tpu_custom_call" | custom-call | flops 40000000 | bytes 10000000 | tf_op jit(solution)/shard_map/pallas_call | solution.py:395
  17.2 0.0 copy-start.1
  17.2 7.2 %all-to-all-start = ((f32[32,8,128]{2,1,0:T(8,128)}), f32[32,8,128]{2,1,0:T(8,128)S(1)}, u32[]{:S(2)}, u32[]{:S(2)}) async-start(f32[32,8,128]{2,1,0:T(8,128)} %shard_map.165), calls=%async_computation | async-start | bytes 262144 | tf_op jit(solution)/shard_map/all_to_all | solution.py:403
  24.4 0.0 collective-permute-done.1.odd_ref
  24.4 0.0 collective-permute-done.even_ref
  24.4 0.0 copy-done.2
  24.4 0.0 copy-done.3
  24.4 0.0 copy-done.4
  24.4 0.0 copy-done.5
  24.4 0.0 copy-done.6
  24.4 0.0 copy-done.7
  24.4 0.0 copy-done.8
  24.5 0.0 copy-done.9
  24.5 0.0 copy-done.1
  24.5 0.0 copy-start
  24.5 0.0 copy-start.12
  24.5 3.3 %shard_map.164 = (f32[128,256]{1,0:T(8,128)S(1)}, bf16[256,128]{1,0:T(8,128)(2,1)S(1)}) custom-call(s32[1]{0:T(128)} %bitcast.refs_0_.first_ref, bf16[256,128]{1,0:T(8,128)(2,1)S(1)} %collective-permute-done.even_ref, bf16[256,128]{1,0:T(8,128)(2,1)S(1)} %copy-done.8, bf16[256,128]{1,0:T(8,128)(2,1)S(1)} %collective-permute-done.1.odd_ref, ...), custom_call_target="tpu_custom_call" | custom-call | flops 2000000000 | bytes 20000000 | tf_op jit(solution)/shard_map/pallas_call | solution.py:413
  27.8 0.0 copy-start.10
  27.9 0.0 copy-start.13
  27.9 4.9 %collective-permute-start.3 = (bf16[256,128]{1,0:T(8,128)(2,1)S(1)}, bf16[256,128]{1,0:T(8,128)(2,1)S(1)}, u32[]{:S(2)}, u32[]{:S(2)}) collective-permute-start(bf16[256,128]{1,0:T(8,128)(2,1)S(1)} %get-tuple-element.14.own_ref), channel_id=1, source_target_pairs={{1,2},{2,1},{3,4},{4,3},{5,6},{6,5},{7,8},{8,7},{9,10},{10,9},{11,... | collective-permute-start | bytes 196616 | tf_op jit(solution)/shard_map/ppermute | solution.py:369
  32.7 1.9 %collective-permute-start.2 = (bf16[256,128]{1,0:T(8,128)(2,1)S(1)}, bf16[256,128]{1,0:T(8,128)(2,1)S(1)}, u32[]{:S(2)}, u32[]{:S(2)}) collective-permute-start(bf16[256,128]{1,0:T(8,128)(2,1)S(1)} %get-tuple-element.14.own_ref), channel_id=1, source_target_pairs={{0,1},{1,0},{2,3},{3,2},{4,5},{5,4},{6,7},{7,6},{8,9},{9,8},{10,11... | collective-permute-start | bytes 196616 | tf_op jit(solution)/shard_map/ppermute | solution.py:369
  34.7 0.0 all-to-all-done.tiles_ref
  34.7 0.0 copy-done
  34.7 0.0 copy-done.12
  34.7 2.9 %shard_map.166.refs_8_ = f32[8,256]{1,0:T(8,128)S(1)} custom-call(s32[1]{0:T(128)} %bitcast.refs_0_.first_ref, f32[32,8,128]{2,1,0:T(8,128)S(1)} %all-to-all-done.tiles_ref, f32[3,256]{1,0:T(4,128)S(1)} %copy-done, s32[2,2,128]{2,1,0:T(2,128)S(1)} %copy-done.12), custom_call_target="tpu_custom_call" | custom-call | flops 80000000 | bytes 16000000 | tf_op jit(solution)/shard_map/pallas_call | solution.py:427
  37.6 0.0 collective-permute-done.3.odd_ref
  37.6 1.3 %collective-permute-done.2.even_ref = bf16[256,128]{1,0:T(8,128)(2,1)S(1)} collective-permute-done((bf16[256,128]{1,0:T(8,128)(2,1)S(1)}, bf16[256,128]{1,0:T(8,128)(2,1)S(1)}, u32[]{:S(2)}, u32[]{:S(2)}) %collective-permute-start.2) | collective-permute-done | bytes 65568 | tf_op jit(solution)/shard_map/ppermute | solution.py:369
  38.9 0.0 copy-done.10
  38.9 0.0 copy-done.13
  38.9 3.9 %shard_map.167 = f32[3,256]{1,0:T(4,128)} custom-call(s32[1]{0:T(128)} %bitcast.refs_0_.first_ref, bf16[256,128]{1,0:T(8,128)(2,1)S(1)} %collective-permute-done.2.even_ref, bf16[256,128]{1,0:T(8,128)(2,1)S(1)} %get-tuple-element.14.own_ref, bf16[256,128]{1,0:T(8,128)(2,1)S(1)} %collective-permute-done.3.odd_ref, ...), custom_call_target="tpu_custom_call" | custom-call | flops 2000000000 | bytes 20000000 | tf_op jit(solution)/shard_map/pallas_call | solution.py:445
Async XLA Ops:
  2.6 13.8 %copy-start.11 = (f32[8,128]{1,0:T(8,128)S(1)}, f32[8,128]{1,0:T(8,128)}, u32[]{:S(2)}) copy-start(f32[8,128]{1,0:T(8,128)} %get-tuple-element.16.tile_ref) | copy-start | bytes 12292
  2.6 21.8 %collective-permute-start.1 = (bf16[256,128]{1,0:T(8,128)(2,1)}, bf16[256,128]{1,0:T(8,128)(2,1)S(1)}, u32[]{:S(2)}, u32[]{:S(2)}) collective-permute-start(bf16[256,128]{1,0:T(8,128)(2,1)} %get-tuple-element.11.own_ref), channel_id=1, source_target_pairs={{1,2},{2,1},{3,4},{4,3},{5,6},{6,5},{7,8},{8,7},{9,10},{10,9},{11,... | collective-permute-start | bytes 196616 | tf_op jit(solution)/shard_map/ppermute | solution.py:369
  13.8 10.5 %collective-permute-start = (bf16[256,128]{1,0:T(8,128)(2,1)}, bf16[256,128]{1,0:T(8,128)(2,1)S(1)}, u32[]{:S(2)}, u32[]{:S(2)}) collective-permute-start(bf16[256,128]{1,0:T(8,128)(2,1)} %get-tuple-element.11.own_ref), channel_id=1, source_target_pairs={{0,1},{1,0},{2,3},{3,2},{4,5},{5,4},{6,7},{7,6},{8,9},{9,8},{10,11... | collective-permute-start | bytes 196616 | tf_op jit(solution)/shard_map/ppermute | solution.py:369
  16.4 8.0 %copy-start.2 = (bf16[2,256,128]{2,1,0:T(8,128)(2,1)S(1)}, bf16[2,256,128]{2,1,0:T(8,128)(2,1)}, u32[]{:S(2)}) copy-start(bf16[2,256,128]{2,1,0:T(8,128)(2,1)} %refs_5_.5) | copy-start | bytes 393220
  16.4 8.0 %copy-start.3 = (f32[128,256]{1,0:T(8,128)S(1)}, f32[128,256]{1,0:T(8,128)}, u32[]{:S(2)}) copy-start(f32[128,256]{1,0:T(8,128)} %get-tuple-element.12.stream_ref) | copy-start | bytes 393220
  16.4 8.0 %copy-start.4 = (bf16[2,128,128]{2,1,0:T(8,128)(2,1)S(1)}, bf16[2,128,128]{2,1,0:T(8,128)(2,1)}, u32[]{:S(2)}) copy-start(bf16[2,128,128]{2,1,0:T(8,128)(2,1)} %refs_0_.3) | copy-start | bytes 196612
  16.5 8.0 %copy-start.5 = (bf16[2,128,128]{2,1,0:T(8,128)(2,1)S(1)}, bf16[2,128,128]{2,1,0:T(8,128)(2,1)}, u32[]{:S(2)}) copy-start(bf16[2,128,128]{2,1,0:T(8,128)(2,1)} %refs_1_.4) | copy-start | bytes 196612
  16.5 8.0 %copy-start.6 = (bf16[2,128,128]{2,1,0:T(8,128)(2,1)S(1)}, bf16[2,128,128]{2,1,0:T(8,128)(2,1)}, u32[]{:S(2)}) copy-start(bf16[2,128,128]{2,1,0:T(8,128)(2,1)} %refs_2_.5) | copy-start | bytes 196612
  16.5 8.0 %copy-start.7 = (bf16[2,128,128]{2,1,0:T(8,128)(2,1)S(1)}, bf16[2,128,128]{2,1,0:T(8,128)(2,1)}, u32[]{:S(2)}) copy-start(bf16[2,128,128]{2,1,0:T(8,128)(2,1)} %refs_3_.5) | copy-start | bytes 196612
  16.5 8.0 %copy-start.8 = (bf16[256,128]{1,0:T(8,128)(2,1)S(1)}, bf16[256,128]{1,0:T(8,128)(2,1)}, u32[]{:S(2)}) copy-start(bf16[256,128]{1,0:T(8,128)(2,1)} %get-tuple-element.11.own_ref) | copy-start | bytes 196612
  16.5 8.0 %copy-start.9 = (f32[8,256]{1,0:T(8,128)S(1)}, f32[8,256]{1,0:T(8,128)}, u32[]{:S(2)}) copy-start(f32[8,256]{1,0:T(8,128)} %get-tuple-element.13.rows_ref) | copy-start | bytes 24580
  17.2 7.3 %copy-start.1 = (bf16[2,128,512]{2,1,0:T(8,128)(2,1)S(1)}, bf16[2,128,512]{2,1,0:T(8,128)(2,1)}, u32[]{:S(2)}) copy-start(bf16[2,128,512]{2,1,0:T(8,128)(2,1)} %refs_4_.5) | copy-start | bytes 786436
  17.2 17.5 %all-to-all-start = ((f32[32,8,128]{2,1,0:T(8,128)}), f32[32,8,128]{2,1,0:T(8,128)S(1)}, u32[]{:S(2)}, u32[]{:S(2)}) async-start(f32[32,8,128]{2,1,0:T(8,128)} %shard_map.165), calls=%async_computation | async-start | bytes 262144 | tf_op jit(solution)/shard_map/all_to_all | solution.py:403
  24.5 10.2 %copy-start = (f32[3,256]{1,0:T(4,128)S(1)}, f32[3,256]{1,0:T(4,128)}, u32[]{:S(2)}) copy-start(f32[3,256]{1,0:T(4,128)} %refs_6_.3) | copy-start | bytes 9220
  24.5 10.2 %copy-start.12 = (s32[2,2,128]{2,1,0:T(2,128)S(1)}, s32[2,2,128]{2,1,0:T(2,128)}, u32[]{:S(2)}) copy-start(s32[2,2,128]{2,1,0:T(2,128)} %bonds_ref.1) | copy-start | bytes 6148
  27.8 11.1 %copy-start.10 = (f32[3,256]{1,0:T(4,128)S(1)}, f32[3,256]{1,0:T(4,128)}, u32[]{:S(2)}) copy-start(f32[3,256]{1,0:T(4,128)} %refs_7_.3) | copy-start | bytes 9220
  27.9 11.0 %copy-start.13 = (f32[3,128]{1,0:T(4,128)S(1)}, f32[3,128]{1,0:T(4,128)}, u32[]{:S(2)}) copy-start(f32[3,128]{1,0:T(4,128)} %refs_9_.1) | copy-start | bytes 4612
  27.9 9.7 %collective-permute-start.3 = (bf16[256,128]{1,0:T(8,128)(2,1)S(1)}, bf16[256,128]{1,0:T(8,128)(2,1)S(1)}, u32[]{:S(2)}, u32[]{:S(2)}) collective-permute-start(bf16[256,128]{1,0:T(8,128)(2,1)S(1)} %get-tuple-element.14.own_ref), channel_id=1, source_target_pairs={{1,2},{2,1},{3,4},{4,3},{5,6},{6,5},{7,8},{8,7},{9,10},{10,9},{11,... | collective-permute-start | bytes 196616 | tf_op jit(solution)/shard_map/ppermute | solution.py:369
  32.7 6.2 %collective-permute-start.2 = (bf16[256,128]{1,0:T(8,128)(2,1)S(1)}, bf16[256,128]{1,0:T(8,128)(2,1)S(1)}, u32[]{:S(2)}, u32[]{:S(2)}) collective-permute-start(bf16[256,128]{1,0:T(8,128)(2,1)S(1)} %get-tuple-element.14.own_ref), channel_id=1, source_target_pairs={{0,1},{1,0},{2,3},{3,2},{4,5},{5,4},{6,7},{7,6},{8,9},{9,8},{10,11... | collective-permute-start | bytes 196616 | tf_op jit(solution)/shard_map/ppermute | solution.py:369

commit v2 on v1

--- a/solution.py
+++ b/solution.py
@@ -315,13 +315,124 @@
     normed_ref[...] = (norm_columns(stream) * gains[:, 2:3]).astype(bf16).T
 
 
-def last_layer_kernel(first_ref, even_ref, own_ref, odd_ref, stream_ref, rows_ref, *refs):
-    weights, (positions_ref, noise_ref, force_ref, w_head_ref) = refs[:6], refs[6:10]
-    out_ref, scratch = refs[10], refs[11:]
-    head_rows = jnp.concatenate([w_head_ref[...], jnp.zeros((1, LANES), f32)], axis=0)
-    stream, columns = layer_values(
-        1, first_ref, (even_ref, own_ref, odd_ref), stream_ref, rows_ref, head_rows, weights, scratch
-    )
+def ready_kernel(own_ref, rows_ref, w_query_ref, w_key_ref, w_value_ref, w_out_ref, w_gate_up_ref, w_down_ref, *refs):
+    marks_ref, bias_ref, query_ref, key_ref, value_ref, value_w, out_w, gate_up_w, down_w = refs
+    layer = 1
+    query_scale = LOG2E * (LANES // HEADS) ** -0.5
+    row_block = lax.broadcasted_iota(jnp.int32, (3 * ROWS, LANES), 0) // LANES
+    lane = lax.broadcasted_iota(jnp.int32, (3 * ROWS, LANES), 1)
+    marks_ref[...] = jnp.where((lane % 16 == row_block) & (lane < 32), 1.0, 0.0).astype(bf16)
+    window = rows_ref[5:6, :LANES]
+    rows = []
+    for chunk in range(6):
+        sides = []
+        for block in range(2):
+            offset = chunk - block
+            if 0 <= offset < 5:
+                lane_id = block * 8 + offset
+                sides.append(jnp.broadcast_to(window[:, lane_id : lane_id + 1], (1, LANES)))
+            else:
+                sides.append(jnp.full((1, LANES), ABSENT, f32))
+        rows.append(jnp.concatenate(sides, axis=1))
+    rows = jnp.concatenate(rows + [jnp.zeros((10, ROWS), f32)], axis=0)
+    high = rows.astype(bf16)
+    low = (rows - high.astype(f32)).astype(bf16)
+    bias_ref[...] = jnp.concatenate([high, low, jnp.zeros((LANES - 32, ROWS), bf16)], axis=0)
+    value_w[...] = w_value_ref[layer].T
+    out_w[...] = w_out_ref[layer].T
+    gate_up_w[...] = w_gate_up_ref[layer].T
+    down_w[...] = w_down_ref[layer].T
+    key_ref[...] = dot(own_ref[...], w_key_ref[layer]).astype(bf16)
+    query_ref[...] = (dot_nt(w_query_ref[layer].T, own_ref[...]) * query_scale).astype(bf16)
+    value_ref[...] = dot_nt(value_w[...], own_ref[...]).astype(bf16)
+
+
+def last_layer_kernel(first_ref, even_ref, odd_ref, stream_ref, rows_ref, w_key_ref, *refs):
+    marks_ref, bias_ref, query_ref, key_ref, value_ref, value_w, out_w, gate_up_w, down_w = refs[:9]
+    positions_ref, noise_ref, force_ref, w_head_ref, out_ref = refs[9:14]
+    near, keys, values, attended = refs[14:]
+    layer = 1
+    head_size = LANES // HEADS
+    left, own, right = (slice(place * ROWS, (place + 1) * ROWS) for place in range(3))
+
+    @pl.when(first_ref[0] % 2 == 0)
+    def _():
+        near[:ROWS, :] = odd_ref[...]
+        near[ROWS:, :] = even_ref[...]
+
+    @pl.when(first_ref[0] % 2 == 1)
+    def _():
+        near[:ROWS, :] = even_ref[...]
+        near[ROWS:, :] = odd_ref[...]
+
+    keys[:, LANES:] = marks_ref[...]
+    keys[own, :LANES] = key_ref[...]
+    key_rows = dot(near[...], w_key_ref[layer]).astype(bf16)
+    keys[left, :LANES] = key_rows[:ROWS]
+    keys[right, :LANES] = key_rows[ROWS:]
+    value_t = dot_nt(value_w[...], near[...]).astype(bf16)
+    for head in range(HEADS):
+        part = slice(head * 32, head * 32 + 32)
+        rows = slice(head * 48, head * 48 + 32)
+        values[rows, left] = value_t[part, :ROWS]
+        values[rows, own] = value_ref[part, :]
+        values[rows, right] = value_t[part, ROWS:]
+        values[head * 48 + 32 : head * 48 + 48, :] = jnp.ones((16, 3 * ROWS), bf16)
+
+    def attend(exact):
+        pieces = []
+        sums = []
+
+        def scores_of(head):
+            parts = []
+            if head:
+                parts.append(jnp.zeros((head * head_size, ROWS), bf16))
+            parts.append(query_ref[head * head_size : (head + 1) * head_size])
+            if head < HEADS - 1:
+                parts.append(jnp.zeros(((HEADS - 1 - head) * head_size, ROWS), bf16))
+            return dot(keys[...], jnp.concatenate(parts + [bias_ref[...]], axis=0))
+
+        following = scores_of(0)
+        for head in range(HEADS):
+            scores = following
+            if head < HEADS - 1:
+                following = scores_of(head + 1)
+            if exact:
+                scores = scores - jnp.max(scores, axis=0, keepdims=True)
+            blank = jnp.zeros((LANES, LANES), bf16)
+            weights_t = jnp.concatenate(
+                [
+                    jnp.concatenate([jnp.exp2(scores[: 5 * LANES, :LANES]).astype(bf16), blank], axis=0),
+                    jnp.concatenate([blank, jnp.exp2(scores[LANES:, LANES:]).astype(bf16)], axis=0),
+                ],
+                axis=1,
+            )
+            mixed = dot(values[head * 48 : (head + 1) * 48, :], weights_t)
+            total = mixed[head_size : head_size + 1]
+            sums.append(total)
+            pieces.append(mixed[:head_size] * (1.0 / total))
+        attended[...] = jnp.concatenate(pieces, axis=0).astype(bf16)
+        return jnp.concatenate(sums, axis=0)
+
+    sums = attend(False)
+    safe = (jnp.min(sums) > 2.0**-80) & (jnp.max(sums) < 2.0**100)
+
+    @pl.when(jnp.logical_not(safe))
+    def _():
+        attend(True)
+
+    columns = jnp.concatenate(
+        [rows_ref[3 + index // 2 : 4 + index // 2, (index % 2) * LANES : (index % 2 + 1) * LANES] for index in range(4)]
+        + [w_head_ref[...], jnp.zeros((1, LANES), f32)],
+        axis=0,
+    ).T
+    now = stream_ref[...] + dot(out_w[...], attended[...])
+    normed = (norm_columns(now) * columns[:, 2 * layer + 1 : 2 * layer + 2]).astype(bf16)
+    gate_up = dot(gate_up_w[...], normed)
+    width = gate_up.shape[0] // 2
+    half, up = 0.5 * gate_up[:width], gate_up[width:]
+    hidden = ((half + half * jnp.tanh(half)) * up).astype(bf16)
+    stream = now + dot(down_w[...], hidden)
     final = norm_columns(stream)
     update = jnp.concatenate(
         [jnp.sum(columns[:, 4 + comp : 5 + comp] * final, axis=0, keepdims=True) for comp in range(3)]
@@ -442,27 +553,37 @@
         compiler_params=pltpu.CompilerParams(vmem_limit_bytes=VMEM_SMALL),
     )(first, tiles, positions, bond_atoms)
 
+    hidden_width = w_gate_up.shape[2]
+    parts = pl.pallas_call(
+        ready_kernel,
+        out_shape=tuple(
+            jax.ShapeDtypeStruct(shape, bf16)
+            for shape in (
+                (3 * rows, LANES),
+                (LANES, rows),
+                (LANES, rows),
+                (rows, LANES),
+                (LANES, rows),
+                (LANES, LANES),
+                (LANES, LANES),
+                (hidden_width, LANES),
+                (LANES, hidden_width // 2),
+            )
+        ),
+        in_specs=[vmem] * 8,
+        out_specs=(vmem,) * 9,
+        cost_estimate=pl.CostEstimate(flops=40_000_000, bytes_accessed=10_000_000, transcendentals=1_000_000),
+        compiler_params=pltpu.CompilerParams(vmem_limit_bytes=VMEM_SMALL),
+    )(normed, schedule, *weights)
     return pl.pallas_call(
         last_layer_kernel,
         out_shape=jax.ShapeDtypeStruct(positions.shape, f32),
-        in_specs=[smem] + [vmem] * 15,
+        in_specs=[smem] + [vmem] * 18,
         out_specs=vmem,
-        scratch_shapes=layer_scratch,
+        scratch_shapes=[pltpu.VMEM((2 * rows, LANES), bf16)] + layer_scratch[1:],
         cost_estimate=layer_cost,
         compiler_params=pltpu.CompilerParams(vmem_limit_bytes=VMEM_SMALL),
-    )(
-        first,
-        even,
-        normed,
-        odd,
-        stream,
-        schedule,
-        *weights,
-        positions,
-        fresh_noise,
-        force,
-        w_head,
-    )
+    )(first, even, odd, stream, schedule, w_key, *parts, positions, fresh_noise, force, w_head)
 
 
 def solution(mesh):

time: 43.2 us -> 43.8 us (1.014)
  local copies, waits for them, and re-layouts: 0.08 us -> 0.76 us
    unnamed x28, local copies, waits for them, and re-layouts: 0.08 us -> 0.76 us
  transfers between devices with their start and end apart: 5 -> 5, of which waited for: 1 -> 1; matrix products, arithmetic and copies ran while one was open for 0% -> 0% of each run, Pallas kernels for 16% -> 17%
where the time goes in v2:
time: 43.8 us; the launch traced here: 43.4 us
  starting transfers between devices  27.1 us (62%)
  Pallas kernels  13 us (30%)
  between operations  1.58 us (4%)
  waiting for transfers between devices  0.96 us (2%)
  local copies, waits for them, and re-layouts  0.76 us (2%)
    ppermute x4, starting transfers between devices, from_neighbours(): return (lax.ppermute(array, 'atom', even), lax.ppermute(array, 'atom', odd))  19.9 us
    all_to_all x1, starting transfers between devices, body(): tiles = lax.all_to_all(packed, 'atom', 0, 0)  7.18 us
    pallas_call x1, Pallas kernels, body(): pl.pallas_call(last_layer_kernel, out_shape=jax.ShapeDtypeStruct(position...  3.86 us
    pallas_call x1, Pallas kernels, body(): pl.pallas_call(first_layer_kernel, out_shape=(jax.ShapeDtypeStruct((LANES...  3.33 us
    pallas_call x1, Pallas kernels, body(): pl.pallas_call(force_kernel, out_shape=jax.ShapeDtypeStruct((8, 2 * LANES...  2.99 us
    pallas_call x1, Pallas kernels, body(): pl.pallas_call(prepare_kernel, out_shape=(jax.ShapeDtypeStruct((LANES, ro...  1.95 us
    ppermute x4, waiting for transfers between devices, from_neighbours(): return (lax.ppermute(array, 'atom', even), lax.ppermute(array, 'atom', odd))  0.96 us
  transfers between devices with their start and end apart: 5, of which 1 were waited for; matrix products, arithmetic and copies ran while one was open for 0% of the time, Pallas kernels for 17%

profile of v2, /device:TPU:6, one launch (start us, length us, event | category | flops | bytes accessed | tf_op | source)
XLA Modules:
  0.0 43.4 jit_solution(13047306539721337452)
XLA Ops:
  0.7 2.0 %shard_map.163 = (f32[128,256]{1,0:T(8,128)}, bf16[256,128]{1,0:T(8,128)(2,1)}, f32[8,256]{1,0:T(8,128)}, f32[8,128]{1,0:T(8,128)}) custom-call(s32[1]{0:T(128)} %bitcast.refs_0_.first_ref, s32[1]{0:T(128)S(6)} %copy.18.refs_1_, f32[3,256]{1,0:T(4,128)} %refs_9_.1, bf16[256,128]{1,0:T(8,128)(2,1)} %refs_3_.2, f32[3,128]{1,0:T(4,128)} %refs_4_.2, ...), custom_call_target="tpu_custom_call" | custom-call | tf_op jit(solution)/shard_map/pallas_call | solution.py:482
  2.6 0.0 copy-start.11
  2.6 11.2 %collective-permute-start.1 = (bf16[256,128]{1,0:T(8,128)(2,1)}, bf16[256,128]{1,0:T(8,128)(2,1)S(1)}, u32[]{:S(2)}, u32[]{:S(2)}) collective-permute-start(bf16[256,128]{1,0:T(8,128)(2,1)} %get-tuple-element.20.own_ref), channel_id=1, source_target_pairs={{1,2},{2,1},{3,4},{4,3},{5,6},{6,5},{7,8},{8,7},{9,10},{10,9},{11,... | collective-permute-start | bytes 196616 | tf_op jit(solution)/shard_map/ppermute | solution.py:480
  13.8 1.9 %collective-permute-start = (bf16[256,128]{1,0:T(8,128)(2,1)}, bf16[256,128]{1,0:T(8,128)(2,1)S(1)}, u32[]{:S(2)}, u32[]{:S(2)}) collective-permute-start(bf16[256,128]{1,0:T(8,128)(2,1)} %get-tuple-element.20.own_ref), channel_id=1, source_target_pairs={{0,1},{1,0},{2,3},{3,2},{4,5},{5,4},{6,7},{7,6},{8,9},{9,8},{10,11... | collective-permute-start | bytes 196616 | tf_op jit(solution)/shard_map/ppermute | solution.py:480
  16.4 0.0 copy-done.11
  16.4 0.0 copy-start.2
  16.4 0.0 copy-start.3
  16.5 0.0 copy-start.4
  16.5 0.0 copy-start.5
  16.5 0.0 copy-start.6
  16.5 0.0 copy-start.7
  16.5 0.0 copy-start.8
  16.5 0.0 copy-start.9
  16.5 0.7 %shard_map.166 = f32[32,8,128]{2,1,0:T(8,128)} custom-call(s32[1]{0:T(128)S(6)} %copy.19.count_ref, f32[8,128]{1,0:T(8,128)S(1)} %copy-done.11), custom_call_target="tpu_custom_call" | custom-call | flops 40000000 | bytes 10000000 | tf_op jit(solution)/shard_map/pallas_call | solution.py:506
  17.2 0.0 copy-start.1
  17.2 7.2 %all-to-all-start = ((f32[32,8,128]{2,1,0:T(8,128)}), f32[32,8,128]{2,1,0:T(8,128)S(1)}, u32[]{:S(2)}, u32[]{:S(2)}) async-start(f32[32,8,128]{2,1,0:T(8,128)} %shard_map.166), calls=%async_computation | async-start | bytes 262144 | tf_op jit(solution)/shard_map/all_to_all | solution.py:514
  24.4 0.0 collective-permute-done.1.odd_ref
  24.4 0.0 collective-permute-done.even_ref
  24.4 0.0 copy-done.2
  24.4 0.0 copy-done.3
  24.4 0.0 copy-done.4
  24.4 0.0 copy-done.5
  24.4 0.0 copy-done.6
  24.4 0.0 copy-done.7
  24.5 0.0 copy-done.8
  24.5 0.0 copy-done.9
  24.5 0.0 copy-done.1
  24.5 3.3 %shard_map.164 = (f32[128,256]{1,0:T(8,128)S(1)}, bf16[256,128]{1,0:T(8,128)(2,1)S(1)}) custom-call(s32[1]{0:T(128)} %bitcast.refs_0_.first_ref, bf16[256,128]{1,0:T(8,128)(2,1)S(1)} %collective-permute-done.even_ref, bf16[256,128]{1,0:T(8,128)(2,1)S(1)} %copy-done.8, bf16[256,128]{1,0:T(8,128)(2,1)S(1)} %collective-permute-done.1.odd_ref, ...), custom_call_target="tpu_custom_call" | custom-call | flops 2000000000 | bytes 20000000 | tf_op jit(solution)/shard_map/pallas_call | solution.py:524
  27.8 0.0 copy-start
  27.8 0.0 copy-start.12
  27.8 4.9 %collective-permute-start.3 = (bf16[256,128]{1,0:T(8,128)(2,1)S(1)}, bf16[256,128]{1,0:T(8,128)(2,1)S(1)}, u32[]{:S(2)}, u32[]{:S(2)}) collective-permute-start(bf16[256,128]{1,0:T(8,128)(2,1)S(1)} %get-tuple-element.23.own_ref), channel_id=1, source_target_pairs={{1,2},{2,1},{3,4},{4,3},{5,6},{6,5},{7,8},{8,7},{9,10},{10,9},{11,... | collective-permute-start | bytes 196616 | tf_op jit(solution)/shard_map/ppermute | solution.py:480
  32.7 1.9 %collective-permute-start.2 = (bf16[256,128]{1,0:T(8,128)(2,1)S(1)}, bf16[256,128]{1,0:T(8,128)(2,1)S(1)}, u32[]{:S(2)}, u32[]{:S(2)}) collective-permute-start(bf16[256,128]{1,0:T(8,128)(2,1)S(1)} %get-tuple-element.23.own_ref), channel_id=1, source_target_pairs={{0,1},{1,0},{2,3},{3,2},{4,5},{5,4},{6,7},{7,6},{8,9},{9,8},{10,11... | collective-permute-start | bytes 196616 | tf_op jit(solution)/shard_map/ppermute | solution.py:480
  34.7 0.2 shard_map.165
  34.9 0.0 all-to-all-done.tiles_ref
  34.9 0.0 copy-done
  34.9 0.0 copy-done.12
  34.9 3.0 %shard_map.167.refs_11_ = f32[8,256]{1,0:T(8,128)S(1)} custom-call(s32[1]{0:T(128)} %bitcast.refs_0_.first_ref, f32[32,8,128]{2,1,0:T(8,128)S(1)} %all-to-all-done.tiles_ref, f32[3,256]{1,0:T(4,128)S(1)} %copy-done, s32[2,2,128]{2,1,0:T(2,128)S(1)} %copy-done.12), custom_call_target="tpu_custom_call" | custom-call | flops 80000000 | bytes 16000000 | tf_op jit(solution)/shard_map/pallas_call | solution.py:538
  37.9 0.0 collective-permute-done.3.odd_ref
  37.9 1.0 %collective-permute-done.2.even_ref = bf16[256,128]{1,0:T(8,128)(2,1)S(1)} collective-permute-done((bf16[256,128]{1,0:T(8,128)(2,1)S(1)}, bf16[256,128]{1,0:T(8,128)(2,1)S(1)}, u32[]{:S(2)}, u32[]{:S(2)}) %collective-permute-start.2) | collective-permute-done | bytes 65568 | tf_op jit(solution)/shard_map/ppermute | solution.py:480
  38.9 0.0 copy-start.10
  38.9 0.0 copy-start.13
  38.9 0.7 %copy-done.10 = f32[3,256]{1,0:T(4,128)S(1)} copy-done((f32[3,256]{1,0:T(4,128)S(1)}, f32[3,256]{1,0:T(4,128)}, u32[]{:S(2)}) %copy-start.10) | copy-done | bytes 3096
  39.6 0.0 copy-done.13
  39.6 3.9 %shard_map.168 = f32[3,256]{1,0:T(4,128)} custom-call(s32[1]{0:T(128)} %bitcast.refs_0_.first_ref, bf16[256,128]{1,0:T(8,128)(2,1)S(1)} %collective-permute-done.2.even_ref, bf16[256,128]{1,0:T(8,128)(2,1)S(1)} %collective-permute-done.3.odd_ref, f32[128,256]{1,0:T(8,128)S(1)} %get-tuple-element.24.stream_ref, f32[8,256]{1,0:T(8,128)S(1)} %copy-done.9, ...), custom_call_target="tpu_custom_call" | custom-call | flops 2000000000 | bytes 20000000 | tf_op jit(solution)/shard_map/pallas_call | solution.py:578
Async XLA Ops:
  2.6 13.8 %copy-start.11 = (f32[8,128]{1,0:T(8,128)S(1)}, f32[8,128]{1,0:T(8,128)}, u32[]{:S(2)}) copy-start(f32[8,128]{1,0:T(8,128)} %get-tuple-element.34.tile_ref) | copy-start | bytes 12292
  2.6 21.8 %collective-permute-start.1 = (bf16[256,128]{1,0:T(8,128)(2,1)}, bf16[256,128]{1,0:T(8,128)(2,1)S(1)}, u32[]{:S(2)}, u32[]{:S(2)}) collective-permute-start(bf16[256,128]{1,0:T(8,128)(2,1)} %get-tuple-element.20.own_ref), channel_id=1, source_target_pairs={{1,2},{2,1},{3,4},{4,3},{5,6},{6,5},{7,8},{8,7},{9,10},{10,9},{11,... | collective-permute-start | bytes 196616 | tf_op jit(solution)/shard_map/ppermute | solution.py:480
  13.8 10.5 %collective-permute-start = (bf16[256,128]{1,0:T(8,128)(2,1)}, bf16[256,128]{1,0:T(8,128)(2,1)S(1)}, u32[]{:S(2)}, u32[]{:S(2)}) collective-permute-start(bf16[256,128]{1,0:T(8,128)(2,1)} %get-tuple-element.20.own_ref), channel_id=1, source_target_pairs={{0,1},{1,0},{2,3},{3,2},{4,5},{5,4},{6,7},{7,6},{8,9},{9,8},{10,11... | collective-permute-start | bytes 196616 | tf_op jit(solution)/shard_map/ppermute | solution.py:480
  16.4 8.0 %copy-start.2 = (bf16[2,256,128]{2,1,0:T(8,128)(2,1)S(1)}, bf16[2,256,128]{2,1,0:T(8,128)(2,1)}, u32[]{:S(2)}) copy-start(bf16[2,256,128]{2,1,0:T(8,128)(2,1)} %w_down_ref.1) | copy-start | bytes 393220
  16.4 8.0 %copy-start.3 = (f32[128,256]{1,0:T(8,128)S(1)}, f32[128,256]{1,0:T(8,128)}, u32[]{:S(2)}) copy-start(f32[128,256]{1,0:T(8,128)} %get-tuple-element.21.stream_ref) | copy-start | bytes 393220
  16.5 8.0 %copy-start.4 = (bf16[2,128,128]{2,1,0:T(8,128)(2,1)S(1)}, bf16[2,128,128]{2,1,0:T(8,128)(2,1)}, u32[]{:S(2)}) copy-start(bf16[2,128,128]{2,1,0:T(8,128)(2,1)} %w_query_ref.1) | copy-start | bytes 196612
  16.5 8.0 %copy-start.5 = (bf16[2,128,128]{2,1,0:T(8,128)(2,1)S(1)}, bf16[2,128,128]{2,1,0:T(8,128)(2,1)}, u32[]{:S(2)}) copy-start(bf16[2,128,128]{2,1,0:T(8,128)(2,1)} %w_value_ref.1) | copy-start | bytes 196612
  16.5 8.0 %copy-start.6 = (bf16[2,128,128]{2,1,0:T(8,128)(2,1)S(1)}, bf16[2,128,128]{2,1,0:T(8,128)(2,1)}, u32[]{:S(2)}) copy-start(bf16[2,128,128]{2,1,0:T(8,128)(2,1)} %w_out_ref.1) | copy-start | bytes 196612
  16.5 8.0 %copy-start.7 = (bf16[2,128,128]{2,1,0:T(8,128)(2,1)S(1)}, bf16[2,128,128]{2,1,0:T(8,128)(2,1)}, u32[]{:S(2)}) copy-start(bf16[2,128,128]{2,1,0:T(8,128)(2,1)} %w_key_ref.3) | copy-start | bytes 196612
  16.5 8.0 %copy-start.8 = (bf16[256,128]{1,0:T(8,128)(2,1)S(1)}, bf16[256,128]{1,0:T(8,128)(2,1)}, u32[]{:S(2)}) copy-start(bf16[256,128]{1,0:T(8,128)(2,1)} %get-tuple-element.20.own_ref) | copy-start | bytes 196612
  16.5 8.0 %copy-start.9 = (f32[8,256]{1,0:T(8,128)S(1)}, f32[8,256]{1,0:T(8,128)}, u32[]{:S(2)}) copy-start(f32[8,256]{1,0:T(8,128)} %get-tuple-element.22.rows_ref) | copy-start | bytes 24580
  17.2 7.3 %copy-start.1 = (bf16[2,128,512]{2,1,0:T(8,128)(2,1)S(1)}, bf16[2,128,512]{2,1,0:T(8,128)(2,1)}, u32[]{:S(2)}) copy-start(bf16[2,128,512]{2,1,0:T(8,128)(2,1)} %w_gate_up_ref.1) | copy-start | bytes 786436
  17.2 17.7 %all-to-all-start = ((f32[32,8,128]{2,1,0:T(8,128)}), f32[32,8,128]{2,1,0:T(8,128)S(1)}, u32[]{:S(2)}, u32[]{:S(2)}) async-start(f32[32,8,128]{2,1,0:T(8,128)} %shard_map.166), calls=%async_computation | async-start | bytes 262144 | tf_op jit(solution)/shard_map/all_to_all | solution.py:514
  27.8 7.1 %copy-start = (f32[3,256]{1,0:T(4,128)S(1)}, f32[3,256]{1,0:T(4,128)}, u32[]{:S(2)}) copy-start(f32[3,256]{1,0:T(4,128)} %refs_9_.1) | copy-start | bytes 9220
  27.8 7.1 %copy-start.12 = (s32[2,2,128]{2,1,0:T(2,128)S(1)}, s32[2,2,128]{2,1,0:T(2,128)}, u32[]{:S(2)}) copy-start(s32[2,2,128]{2,1,0:T(2,128)} %bonds_ref.1) | copy-start | bytes 6148
  27.8 10.1 %collective-permute-start.3 = (bf16[256,128]{1,0:T(8,128)(2,1)S(1)}, bf16[256,128]{1,0:T(8,128)(2,1)S(1)}, u32[]{:S(2)}, u32[]{:S(2)}) collective-permute-start(bf16[256,128]{1,0:T(8,128)(2,1)S(1)} %get-tuple-element.23.own_ref), channel_id=1, source_target_pairs={{1,2},{2,1},{3,4},{4,3},{5,6},{6,5},{7,8},{8,7},{9,10},{10,9},{11,... | collective-permute-start | bytes 196616 | tf_op jit(solution)/shard_map/ppermute | solution.py:480
  32.7 6.2 %collective-permute-start.2 = (bf16[256,128]{1,0:T(8,128)(2,1)S(1)}, bf16[256,128]{1,0:T(8,128)(2,1)S(1)}, u32[]{:S(2)}, u32[]{:S(2)}) collective-permute-start(bf16[256,128]{1,0:T(8,128)(2,1)S(1)} %get-tuple-element.23.own_ref), channel_id=1, source_target_pairs={{0,1},{1,0},{2,3},{3,2},{4,5},{5,4},{6,7},{7,6},{8,9},{9,8},{10,11... | collective-permute-start | bytes 196616 | tf_op jit(solution)/shard_map/ppermute | solution.py:480
  38.9 0.7 %copy-start.10 = (f32[3,256]{1,0:T(4,128)S(1)}, f32[3,256]{1,0:T(4,128)}, u32[]{:S(2)}) copy-start(f32[3,256]{1,0:T(4,128)} %refs_10_.1) | copy-start | bytes 9220
  38.9 0.7 %copy-start.13 = (f32[3,128]{1,0:T(4,128)S(1)}, f32[3,128]{1,0:T(4,128)}, u32[]{:S(2)}) copy-start(f32[3,128]{1,0:T(4,128)} %refs_12_.1) | copy-start | bytes 4612

commit v3 on v1

--- a/solution.py
+++ b/solution.py
@@ -205,7 +205,7 @@
     normed_ref[...] = (norm_columns(stream) * columns[:, 3:4]).astype(bf16).T
 
 
-def layer_values(layer, first_ref, halo, stream_ref, rows_ref, head_rows, weights, scratch):
+def run_layer(layer, first_ref, halo, stream_ref, rows_ref, head_rows, weights, scratch, finish):
     even_ref, own_ref, odd_ref = halo
     w_query_ref, w_key_ref, w_value_ref, w_out_ref, w_gate_up_ref, w_down_ref = weights
     near, keys, values, attended = scratch
@@ -285,56 +285,64 @@
         attended[...] = jnp.concatenate(pieces, axis=0).astype(bf16)
         return jnp.concatenate(sums, axis=0)
 
-    sums = attend(False)
-    safe = (jnp.min(sums) > 2.0**-80) & (jnp.max(sums) < 2.0**100)
-
-    @pl.when(jnp.logical_not(safe))
-    def _():
-        attend(True)
-
     gains = jnp.concatenate(
         [rows_ref[3 + index // 2 : 4 + index // 2, (index % 2) * LANES : (index % 2 + 1) * LANES] for index in range(4)]
         + [head_rows],
         axis=0,
     ).T
-    now = stream_ref[...] + dot(w_out_ref[layer].T, attended[...])
-    normed = (norm_columns(now) * gains[:, 2 * layer + 1 : 2 * layer + 2]).astype(bf16)
-    gate_up = dot(w_gate_up_ref[layer].T, normed)
-    width = gate_up.shape[0] // 2
-    half, up = 0.5 * gate_up[:width], gate_up[width:]
-    hidden = ((half + half * jnp.tanh(half)) * up).astype(bf16)
-    return now + dot(w_down_ref[layer].T, hidden), gains
+    def run(exact):
+        sums = attend(exact)
+        now = stream_ref[...] + dot(w_out_ref[layer].T, attended[...])
+        normed = (norm_columns(now) * gains[:, 2 * layer + 1 : 2 * layer + 2]).astype(bf16)
+        gate_up = dot(w_gate_up_ref[layer].T, normed)
+        width = gate_up.shape[0] // 2
+        half, up = 0.5 * gate_up[:width], gate_up[width:]
+        hidden = ((half + half * jnp.tanh(half)) * up).astype(bf16)
+        finish(now + dot(w_down_ref[layer].T, hidden), gains)
+        return sums
+
+    sums = run(False)
+    safe = (jnp.min(sums) > 2.0**-80) & (jnp.max(sums) < 2.0**100)
+
+    @pl.when(jnp.logical_not(safe))
+    def _():
+        run(True)
 
 
 def first_layer_kernel(first_ref, even_ref, own_ref, odd_ref, stream_ref, rows_ref, *refs):
     weights, (out_ref, normed_ref), scratch = refs[:6], refs[6:8], refs[8:]
-    stream, gains = layer_values(
-        0, first_ref, (even_ref, own_ref, odd_ref), stream_ref, rows_ref, jnp.zeros((4, LANES), f32), weights, scratch
-    )
-    out_ref[...] = stream
-    normed_ref[...] = (norm_columns(stream) * gains[:, 2:3]).astype(bf16).T
+
+    def finish(stream, columns):
+        out_ref[...] = stream
+        normed_ref[...] = (norm_columns(stream) * columns[:, 2:3]).astype(bf16).T
+
+    halo = (even_ref, own_ref, odd_ref)
+    run_layer(0, first_ref, halo, stream_ref, rows_ref, jnp.zeros((4, LANES), f32), weights, scratch, finish)
 
 
 def last_layer_kernel(first_ref, even_ref, own_ref, odd_ref, stream_ref, rows_ref, *refs):
     weights, (positions_ref, noise_ref, force_ref, w_head_ref) = refs[:6], refs[6:10]
     out_ref, scratch = refs[10], refs[11:]
-    head_rows = jnp.concatenate([w_head_ref[...], jnp.zeros((1, LANES), f32)], axis=0)
-    stream, columns = layer_values(
-        1, first_ref, (even_ref, own_ref, odd_ref), stream_ref, rows_ref, head_rows, weights, scratch
-    )
-    final = norm_columns(stream)
-    update = jnp.concatenate(
-        [jnp.sum(columns[:, 4 + comp : 5 + comp] * final, axis=0, keepdims=True) for comp in range(3)]
-        + [jnp.zeros((5, ROWS), f32)],
-        axis=0,
-    )
     level, spread_sq, c_input = rows_ref[0:1], rows_ref[1:2], rows_ref[2:3]
     positions = jnp.concatenate([positions_ref[...], jnp.zeros((5, ROWS), f32)], axis=0)
     fresh = jnp.concatenate([noise_ref[...], jnp.zeros((5, ROWS), f32)], axis=0)
-    denoised = positions * (1.0 / spread_sq) + (level * c_input) * update
-    following = 0.85 * level
-    result = denoised + STEER * force_ref[...] + following * (0.8 * (positions - denoised) / level + 0.6 * fresh)
-    out_ref[...] = result[:3]
+
+    def finish(stream, columns):
+        final = norm_columns(stream)
+        update = jnp.concatenate(
+            [jnp.sum(columns[:, 4 + comp : 5 + comp] * final, axis=0, keepdims=True) for comp in range(3)]
+            + [jnp.zeros((5, ROWS), f32)],
+            axis=0,
+        )
+        denoised = positions * (1.0 / spread_sq) + (level * c_input) * update
+        following = 0.85 * level
+        result = denoised + STEER * force_ref[...]
+        result = result + following * (0.8 * (positions - denoised) / level + 0.6 * fresh)
+        out_ref[...] = result[:3]
+
+    halo = (even_ref, own_ref, odd_ref)
+    head_rows = jnp.concatenate([w_head_ref[...], jnp.zeros((1, LANES), f32)], axis=0)
+    run_layer(1, first_ref, halo, stream_ref, rows_ref, head_rows, weights, scratch, finish)
 
 
 def body(

time: 43.2 us -> 44.4 us (1.028)
  Pallas kernels: 12.7 us -> 13.5 us
  waiting for transfers between devices: 1.3 us -> 1.75 us
    pallas_call x1, Pallas kernels: 3.34 us -> 3.96 us  [body(): pl.pallas_call(first_layer_kernel, out_shape=(jax.ShapeDtypeStruct((LANES...]
    pallas_call x1, Pallas kernels: 3.91 us -> 4.48 us  [body(): pl.pallas_call(last_layer_kernel, out_shape=jax.ShapeDtypeStruct(position...]
    pallas_call x1, Pallas kernels: 2.9 us -> 2.45 us  [body(): pl.pallas_call(force_kernel, out_shape=jax.ShapeDtypeStruct((8, 2 * LANES...]
    ppermute x4, waiting for transfers between devices: 1.29 us -> 1.74 us  [from_neighbours(): return (lax.ppermute(array, 'atom', even), lax.ppermute(array, 'atom', odd))]
where the time goes in v3:
time: 44.4 us; the launch traced here: 44 us
  starting transfers between devices  27.1 us (61%)
  Pallas kernels  13.5 us (30%)
  waiting for transfers between devices  1.75 us (4%)
  between operations  1.59 us (4%)
    ppermute x4, starting transfers between devices, from_neighbours(): return (lax.ppermute(array, 'atom', even), lax.ppermute(array, 'atom', odd))  19.9 us
    all_to_all x1, starting transfers between devices, body(): tiles = lax.all_to_all(packed, 'atom', 0, 0)  7.18 us
    pallas_call x1, Pallas kernels, body(): pl.pallas_call(last_layer_kernel, out_shape=jax.ShapeDtypeStruct(position...  4.48 us
    pallas_call x1, Pallas kernels, body(): pl.pallas_call(first_layer_kernel, out_shape=(jax.ShapeDtypeStruct((LANES...  3.96 us
    pallas_call x1, Pallas kernels, body(): pl.pallas_call(force_kernel, out_shape=jax.ShapeDtypeStruct((8, 2 * LANES...  2.45 us
    pallas_call x1, Pallas kernels, body(): pl.pallas_call(prepare_kernel, out_shape=(jax.ShapeDtypeStruct((LANES, ro...  1.94 us
    ppermute x4, waiting for transfers between devices, from_neighbours(): return (lax.ppermute(array, 'atom', even), lax.ppermute(array, 'atom', odd))  1.74 us
  transfers between devices with their start and end apart: 5, of which 1 were waited for; matrix products, arithmetic and copies ran while one was open for 0% of the time, Pallas kernels for 16%

profile of v3, /device:TPU:6, one launch (start us, length us, event | category | flops | bytes accessed | tf_op | source)
XLA Modules:
  0.0 44.0 jit_solution(12396317941264809932)
XLA Ops:
  0.7 1.9 %shard_map.163 = (f32[128,256]{1,0:T(8,128)}, bf16[256,128]{1,0:T(8,128)(2,1)}, f32[8,256]{1,0:T(8,128)}, f32[8,128]{1,0:T(8,128)}) custom-call(s32[1]{0:T(128)} %bitcast.refs_0_.first_ref, s32[1]{0:T(128)S(6)} %copy.18.refs_1_, f32[3,256]{1,0:T(4,128)} %refs_6_.3, bf16[256,128]{1,0:T(8,128)(2,1)} %refs_3_.3, f32[3,128]{1,0:T(4,128)} %refs_4_.3, ...), custom_call_target="tpu_custom_call" | custom-call | tf_op jit(solution)/shard_map/pallas_call | solution.py:379
  2.6 0.0 copy-start.11
  2.6 11.2 %collective-permute-start.1 = (bf16[256,128]{1,0:T(8,128)(2,1)}, bf16[256,128]{1,0:T(8,128)(2,1)S(1)}, u32[]{:S(2)}, u32[]{:S(2)}) collective-permute-start(bf16[256,128]{1,0:T(8,128)(2,1)} %get-tuple-element.11.own_ref), channel_id=1, source_target_pairs={{1,2},{2,1},{3,4},{4,3},{5,6},{6,5},{7,8},{8,7},{9,10},{10,9},{11,... | collective-permute-start | bytes 196616 | tf_op jit(solution)/shard_map/ppermute | solution.py:377
  13.8 1.9 %collective-permute-start = (bf16[256,128]{1,0:T(8,128)(2,1)}, bf16[256,128]{1,0:T(8,128)(2,1)S(1)}, u32[]{:S(2)}, u32[]{:S(2)}) collective-permute-start(bf16[256,128]{1,0:T(8,128)(2,1)} %get-tuple-element.11.own_ref), channel_id=1, source_target_pairs={{0,1},{1,0},{2,3},{3,2},{4,5},{5,4},{6,7},{7,6},{8,9},{9,8},{10,11... | collective-permute-start | bytes 196616 | tf_op jit(solution)/shard_map/ppermute | solution.py:377
  16.4 0.0 copy-done.11
  16.4 0.0 copy-start.2
  16.4 0.0 copy-start.3
  16.4 0.0 copy-start.4
  16.5 0.0 copy-start.5
  16.5 0.0 copy-start.6
  16.5 0.0 copy-start.7
  16.5 0.0 copy-start.8
  16.5 0.0 copy-start.9
  16.5 0.7 %shard_map.165 = f32[32,8,128]{2,1,0:T(8,128)} custom-call(s32[1]{0:T(128)S(6)} %copy.19.count_ref, f32[8,128]{1,0:T(8,128)S(1)} %copy-done.11), custom_call_target="tpu_custom_call" | custom-call | flops 40000000 | bytes 10000000 | tf_op jit(solution)/shard_map/pallas_call | solution.py:403
  17.2 0.0 copy-start.1
  17.2 7.2 %all-to-all-start = ((f32[32,8,128]{2,1,0:T(8,128)}), f32[32,8,128]{2,1,0:T(8,128)S(1)}, u32[]{:S(2)}, u32[]{:S(2)}) async-start(f32[32,8,128]{2,1,0:T(8,128)} %shard_map.165), calls=%async_computation | async-start | bytes 262144 | tf_op jit(solution)/shard_map/all_to_all | solution.py:411
  24.4 0.0 collective-permute-done.1.odd_ref
  24.4 0.0 collective-permute-done.even_ref
  24.4 0.0 copy-done.2
  24.4 0.0 copy-done.3
  24.4 0.0 copy-done.4
  24.4 0.0 copy-done.5
  24.4 0.0 copy-done.6
  24.4 0.0 copy-done.7
  24.4 0.0 copy-done.8
  24.5 0.0 copy-done.9
  24.5 0.0 copy-done.1
  24.5 0.0 copy-start
  24.5 0.0 copy-start.12
  24.5 4.0 %shard_map.164 = (f32[128,256]{1,0:T(8,128)S(1)}, bf16[256,128]{1,0:T(8,128)(2,1)S(1)}) custom-call(s32[1]{0:T(128)} %bitcast.refs_0_.first_ref, bf16[256,128]{1,0:T(8,128)(2,1)S(1)} %collective-permute-done.even_ref, bf16[256,128]{1,0:T(8,128)(2,1)S(1)} %copy-done.8, bf16[256,128]{1,0:T(8,128)(2,1)S(1)} %collective-permute-done.1.odd_ref, ...), custom_call_target="tpu_custom_call" | custom-call | flops 2000000000 | bytes 20000000 | tf_op jit(solution)/shard_map/pallas_call | solution.py:421
  28.5 0.0 copy-start.10
  28.5 0.0 copy-start.13
  28.5 4.9 %collective-permute-start.3 = (bf16[256,128]{1,0:T(8,128)(2,1)S(1)}, bf16[256,128]{1,0:T(8,128)(2,1)S(1)}, u32[]{:S(2)}, u32[]{:S(2)}) collective-permute-start(bf16[256,128]{1,0:T(8,128)(2,1)S(1)} %get-tuple-element.14.own_ref), channel_id=1, source_target_pairs={{1,2},{2,1},{3,4},{4,3},{5,6},{6,5},{7,8},{8,7},{9,10},{10,9},{11,... | collective-permute-start | bytes 196616 | tf_op jit(solution)/shard_map/ppermute | solution.py:377
  33.4 1.9 %collective-permute-start.2 = (bf16[256,128]{1,0:T(8,128)(2,1)S(1)}, bf16[256,128]{1,0:T(8,128)(2,1)S(1)}, u32[]{:S(2)}, u32[]{:S(2)}) collective-permute-start(bf16[256,128]{1,0:T(8,128)(2,1)S(1)} %get-tuple-element.14.own_ref), channel_id=1, source_target_pairs={{0,1},{1,0},{2,3},{3,2},{4,5},{5,4},{6,7},{7,6},{8,9},{9,8},{10,11... | collective-permute-start | bytes 196616 | tf_op jit(solution)/shard_map/ppermute | solution.py:377
  35.3 0.0 all-to-all-done.tiles_ref
  35.3 0.0 copy-done
  35.3 0.0 copy-done.12
  35.3 2.4 %shard_map.166.refs_8_ = f32[8,256]{1,0:T(8,128)S(1)} custom-call(s32[1]{0:T(128)} %bitcast.refs_0_.first_ref, f32[32,8,128]{2,1,0:T(8,128)S(1)} %all-to-all-done.tiles_ref, f32[3,256]{1,0:T(4,128)S(1)} %copy-done, s32[2,2,128]{2,1,0:T(2,128)S(1)} %copy-done.12), custom_call_target="tpu_custom_call" | custom-call | flops 80000000 | bytes 16000000 | tf_op jit(solution)/shard_map/pallas_call | solution.py:435
  37.8 0.0 collective-permute-done.3.odd_ref
  37.8 1.7 %collective-permute-done.2.even_ref = bf16[256,128]{1,0:T(8,128)(2,1)S(1)} collective-permute-done((bf16[256,128]{1,0:T(8,128)(2,1)S(1)}, bf16[256,128]{1,0:T(8,128)(2,1)S(1)}, u32[]{:S(2)}, u32[]{:S(2)}) %collective-permute-start.2) | collective-permute-done | bytes 65568 | tf_op jit(solution)/shard_map/ppermute | solution.py:377
  39.5 0.0 copy-done.10
  39.5 0.0 copy-done.13
  39.5 4.5 %shard_map.167 = f32[3,256]{1,0:T(4,128)} custom-call(s32[1]{0:T(128)} %bitcast.refs_0_.first_ref, bf16[256,128]{1,0:T(8,128)(2,1)S(1)} %collective-permute-done.2.even_ref, bf16[256,128]{1,0:T(8,128)(2,1)S(1)} %get-tuple-element.14.own_ref, bf16[256,128]{1,0:T(8,128)(2,1)S(1)} %collective-permute-done.3.odd_ref, ...), custom_call_target="tpu_custom_call" | custom-call | flops 2000000000 | bytes 20000000 | tf_op jit(solution)/shard_map/pallas_call | solution.py:453
Async XLA Ops:
  2.6 13.8 %copy-start.11 = (f32[8,128]{1,0:T(8,128)S(1)}, f32[8,128]{1,0:T(8,128)}, u32[]{:S(2)}) copy-start(f32[8,128]{1,0:T(8,128)} %get-tuple-element.16.tile_ref) | copy-start | bytes 12292
  2.6 21.8 %collective-permute-start.1 = (bf16[256,128]{1,0:T(8,128)(2,1)}, bf16[256,128]{1,0:T(8,128)(2,1)S(1)}, u32[]{:S(2)}, u32[]{:S(2)}) collective-permute-start(bf16[256,128]{1,0:T(8,128)(2,1)} %get-tuple-element.11.own_ref), channel_id=1, source_target_pairs={{1,2},{2,1},{3,4},{4,3},{5,6},{6,5},{7,8},{8,7},{9,10},{10,9},{11,... | collective-permute-start | bytes 196616 | tf_op jit(solution)/shard_map/ppermute | solution.py:377
  13.8 10.5 %collective-permute-start = (bf16[256,128]{1,0:T(8,128)(2,1)}, bf16[256,128]{1,0:T(8,128)(2,1)S(1)}, u32[]{:S(2)}, u32[]{:S(2)}) collective-permute-start(bf16[256,128]{1,0:T(8,128)(2,1)} %get-tuple-element.11.own_ref), channel_id=1, source_target_pairs={{0,1},{1,0},{2,3},{3,2},{4,5},{5,4},{6,7},{7,6},{8,9},{9,8},{10,11... | collective-permute-start | bytes 196616 | tf_op jit(solution)/shard_map/ppermute | solution.py:377
  16.4 8.0 %copy-start.2 = (bf16[2,256,128]{2,1,0:T(8,128)(2,1)S(1)}, bf16[2,256,128]{2,1,0:T(8,128)(2,1)}, u32[]{:S(2)}) copy-start(bf16[2,256,128]{2,1,0:T(8,128)(2,1)} %refs_5_.5) | copy-start | bytes 393220
  16.4 8.0 %copy-start.3 = (f32[128,256]{1,0:T(8,128)S(1)}, f32[128,256]{1,0:T(8,128)}, u32[]{:S(2)}) copy-start(f32[128,256]{1,0:T(8,128)} %get-tuple-element.12.stream_ref) | copy-start | bytes 393220
  16.4 8.0 %copy-start.4 = (bf16[2,128,128]{2,1,0:T(8,128)(2,1)S(1)}, bf16[2,128,128]{2,1,0:T(8,128)(2,1)}, u32[]{:S(2)}) copy-start(bf16[2,128,128]{2,1,0:T(8,128)(2,1)} %refs_0_.3) | copy-start | bytes 196612
  16.5 8.0 %copy-start.5 = (bf16[2,128,128]{2,1,0:T(8,128)(2,1)S(1)}, bf16[2,128,128]{2,1,0:T(8,128)(2,1)}, u32[]{:S(2)}) copy-start(bf16[2,128,128]{2,1,0:T(8,128)(2,1)} %refs_1_.4) | copy-start | bytes 196612
  16.5 8.0 %copy-start.6 = (bf16[2,128,128]{2,1,0:T(8,128)(2,1)S(1)}, bf16[2,128,128]{2,1,0:T(8,128)(2,1)}, u32[]{:S(2)}) copy-start(bf16[2,128,128]{2,1,0:T(8,128)(2,1)} %refs_2_.5) | copy-start | bytes 196612
  16.5 8.0 %copy-start.7 = (bf16[2,128,128]{2,1,0:T(8,128)(2,1)S(1)}, bf16[2,128,128]{2,1,0:T(8,128)(2,1)}, u32[]{:S(2)}) copy-start(bf16[2,128,128]{2,1,0:T(8,128)(2,1)} %refs_3_.5) | copy-start | bytes 196612
  16.5 8.0 %copy-start.8 = (bf16[256,128]{1,0:T(8,128)(2,1)S(1)}, bf16[256,128]{1,0:T(8,128)(2,1)}, u32[]{:S(2)}) copy-start(bf16[256,128]{1,0:T(8,128)(2,1)} %get-tuple-element.11.own_ref) | copy-start | bytes 196612
  16.5 8.0 %copy-start.9 = (f32[8,256]{1,0:T(8,128)S(1)}, f32[8,256]{1,0:T(8,128)}, u32[]{:S(2)}) copy-start(f32[8,256]{1,0:T(8,128)} %get-tuple-element.13.rows_ref) | copy-start | bytes 24580
  17.2 7.3 %copy-start.1 = (bf16[2,128,512]{2,1,0:T(8,128)(2,1)S(1)}, bf16[2,128,512]{2,1,0:T(8,128)(2,1)}, u32[]{:S(2)}) copy-start(bf16[2,128,512]{2,1,0:T(8,128)(2,1)} %refs_4_.5) | copy-start | bytes 786436
  17.2 18.1 %all-to-all-start = ((f32[32,8,128]{2,1,0:T(8,128)}), f32[32,8,128]{2,1,0:T(8,128)S(1)}, u32[]{:S(2)}, u32[]{:S(2)}) async-start(f32[32,8,128]{2,1,0:T(8,128)} %shard_map.165), calls=%async_computation | async-start | bytes 262144 | tf_op jit(solution)/shard_map/all_to_all | solution.py:411
  24.5 10.8 %copy-start = (f32[3,256]{1,0:T(4,128)S(1)}, f32[3,256]{1,0:T(4,128)}, u32[]{:S(2)}) copy-start(f32[3,256]{1,0:T(4,128)} %refs_6_.3) | copy-start | bytes 9220
  24.5 10.8 %copy-start.12 = (s32[2,2,128]{2,1,0:T(2,128)S(1)}, s32[2,2,128]{2,1,0:T(2,128)}, u32[]{:S(2)}) copy-start(s32[2,2,128]{2,1,0:T(2,128)} %bonds_ref.1) | copy-start | bytes 6148
  28.5 11.1 %copy-start.10 = (f32[3,256]{1,0:T(4,128)S(1)}, f32[3,256]{1,0:T(4,128)}, u32[]{:S(2)}) copy-start(f32[3,256]{1,0:T(4,128)} %refs_7_.3) | copy-start | bytes 9220
  28.5 11.0 %copy-start.13 = (f32[3,128]{1,0:T(4,128)S(1)}, f32[3,128]{1,0:T(4,128)}, u32[]{:S(2)}) copy-start(f32[3,128]{1,0:T(4,128)} %refs_9_.1) | copy-start | bytes 4612
  28.5 9.3 %collective-permute-start.3 = (bf16[256,128]{1,0:T(8,128)(2,1)S(1)}, bf16[256,128]{1,0:T(8,128)(2,1)S(1)}, u32[]{:S(2)}, u32[]{:S(2)}) collective-permute-start(bf16[256,128]{1,0:T(8,128)(2,1)S(1)} %get-tuple-element.14.own_ref), channel_id=1, source_target_pairs={{1,2},{2,1},{3,4},{4,3},{5,6},{6,5},{7,8},{8,7},{9,10},{10,9},{11,... | collective-permute-start | bytes 196616 | tf_op jit(solution)/shard_map/ppermute | solution.py:377
  33.4 6.2 %collective-permute-start.2 = (bf16[256,128]{1,0:T(8,128)(2,1)S(1)}, bf16[256,128]{1,0:T(8,128)(2,1)S(1)}, u32[]{:S(2)}, u32[]{:S(2)}) collective-permute-start(bf16[256,128]{1,0:T(8,128)(2,1)S(1)} %get-tuple-element.14.own_ref), channel_id=1, source_target_pairs={{0,1},{1,0},{2,3},{3,2},{4,5},{5,4},{6,7},{7,6},{8,9},{9,8},{10,11... | collective-permute-start | bytes 196616 | tf_op jit(solution)/shard_map/ppermute | solution.py:377
